TPU v7x, 32 devices: a whole 2x2x4 slice. The times are simulated.
32 devices in a mesh: head: 2 (over y), fsdp: 16 (over z, x, core).
Axes of the slice: x: 2, y: 2, z: 4, core: 2. Of those that a mesh axis runs over, the one named last changes fastest.
Arguments:
- tokens: float32 [16, 256, 2304], P('fsdp', 'head'), may hold values from -8 to 8
- cotangent: float32 [16, 256, 2304], P('fsdp', 'head'), may hold values from -6 to 6
- gains: float32 [4, 2304], P(None, ('head', 'fsdp')), may hold values from -0.3 to 0.3
- gains_first: float32 [4, 2304], P(None, ('head', 'fsdp')), may hold values from -40 to 40
- gains_second: float32 [4, 2304], P(None, ('head', 'fsdp')), may hold values from 106.496 to 1720.32
- attn_weight: float32 [3, 2048, 2304], P(None, ('head', 'fsdp')), may hold values from -0.133680556 to 0.133680556
- attn_first: float32 [3, 2048, 2304], P(None, ('head', 'fsdp')), may hold values from -28 to 28
- attn_second: float32 [3, 2048, 2304], P(None, ('head', 'fsdp')), may hold values from 27.0336 to 1720.32
- ffn_weight: float32 [9216, 3, 2304], P(('head', 'fsdp')), may hold values from -0.125 to 0.125
- ffn_first: float32 [9216, 3, 2304], P(('head', 'fsdp')), may hold values from -40 to 40
- ffn_second: float32 [9216, 3, 2304], P(('head', 'fsdp')), may hold values from 106.496 to 1720.32
Outputs:
- output: float32 [16, 256, 2304], P('fsdp', 'head')
- tokens_grad: float32 [16, 256, 2304], P('fsdp', 'head')
- gains_first_new: float32 [4, 2304], P(None, ('head', 'fsdp'))
- gains_second_new: float32 [4, 2304], P(None, ('head', 'fsdp'))
- gains_new: float32 [4, 2304], P(None, ('head', 'fsdp'))
- attn_first_new: float32 [3, 2048, 2304], P(None, ('head', 'fsdp'))
- attn_second_new: float32 [3, 2048, 2304], P(None, ('head', 'fsdp'))
- attn_weight_new: float32 [3, 2048, 2304], P(None, ('head', 'fsdp'))
- ffn_first_new: float32 [9216, 3, 2304], P(('head', 'fsdp'))
- ffn_second_new: float32 [9216, 3, 2304], P(('head', 'fsdp'))
- ffn_weight_new: float32 [9216, 3, 2304], P(('head', 'fsdp'))
All inputs are finite; a program needn't handle non-finite values.
Results may differ from a plain program's by a relative error of at most 0.023.
Values may be sent and summed in bfloat16 or wider, within the bound.
A program may use at most 576 MiB of HBM per device.

v0:
```python
import functools
import math

import jax
import jax.numpy as jnp
import numpy as np
from jax import lax
from jax.experimental import pallas as pl
from jax.experimental.pallas import tpu as pltpu
from jax.sharding import PartitionSpec as P

HQ = 8
HK = 4
HD = 256
WIN = 4096
STEP = 10
SEQ_LEN = 8192


eps_norm = 1e-06
softcap = 50.0
beta_one = 0.9
beta_two = 0.95
adam_eps = 1e-08
rate_matrix = 0.02
rate_gain = 0.2
decay_matrix = 0.1

bfloat = jnp.bfloat16
single = jnp.float32
MESH = pl.DeviceIdType.MESH


def norm_scale(values, scales):
    return (
        values
        * lax.rsqrt(jnp.mean(values * values, axis=-1, keepdims=True) + eps_norm)
        * (1.0 + scales)
    )


def turn_angles(positions, head_width):
    halfway = head_width // 2
    inverse_freq = 10000.0 ** (-(jnp.arange(halfway, dtype=jnp.float32) * 2.0) / head_width)
    return positions.astype(jnp.float32)[:, None] * inverse_freq[None, :]


def rotate(values, angles, direction):
    halfway = values.shape[-1] // 2
    cosine = jnp.cos(angles)[:, None, :]
    sine_part = direction * jnp.sin(angles)[:, None, :]
    former = values[..., :halfway]
    latter = values[..., halfway:]
    return jnp.concatenate(
        [former * cosine - latter * sine_part, latter * cosine + former * sine_part], axis=-1
    )


def adamw(weight, moment, second, gradient, step_rate, decay_rate):
    moment = beta_one * moment + (1.0 - beta_one) * gradient
    second = beta_two * second + (1.0 - beta_two) * gradient * gradient
    update = (
        moment / (1.0 - beta_one**STEP) / (jnp.sqrt(second / (1.0 - beta_two**STEP)) + adam_eps)
        + decay_rate * weight
    )
    return (moment, second, weight - step_rate * update)


def hidden_unit(gate_part, up_part):
    return jax.nn.gelu(gate_part, approximate=True) * up_part


def ring_of(chip, chips):
    wide = chips // 4
    deep, side = chip // wide, chip % wide
    return side * 4 + deep + (side % 2) * (3 - 2 * deep)


def chip_of(ring, chips):
    wide = chips // 4
    side, along = ring // 4, ring % 4
    return (along + (side % 2) * (3 - 2 * along)) * wide + side


def ring_places(chips):
    index = lax.axis_index("fsdp")
    core, chip = index % 2, index // 2
    ring = ring_of(chip, chips)
    right = 2 * chip_of((ring + 1) % chips, chips) + core
    left = 2 * chip_of((ring + chips - 1) % chips, chips) + core
    return chip, ring, right, left


def ring_barrier(right, left):
    barrier = pltpu.get_barrier_semaphore()
    for neighbour in (left, right):
        pl.semaphore_signal(barrier, inc=1, device_id={"fsdp": neighbour}, device_id_type=MESH)
    pl.semaphore_wait(barrier, 2)


def region(shape, pieces, way, piece):
    rows, columns = shape
    if rows % 32 == 0:
        size = rows // 2 // pieces
        start = way * (rows // 2) + piece * size
        return (pl.ds(start, size), pl.ds(0, columns)), (pl.ds(piece * size, size), pl.ds(0, columns))
    size = columns // 2
    return (pl.ds(0, rows), pl.ds(way * size, size)), (pl.ds(0, rows), pl.ds(0, size))


def half_shape(rows, columns):
    return (rows // 2, columns) if rows % 32 == 0 else (rows, columns // 2)


def gather_kernel(chips, pieces, own_ref, all_ref, local_sem, send_sem, recv_sem):
    chip, ring, right, left = ring_places(chips)
    ring_barrier(right, left)
    keep = pltpu.make_async_copy(own_ref, all_ref.at[chip], local_sem)
    keep.start()

    def copy(way, step, piece, first):
        owner = chip_of((ring + (chips - step if way == 0 else step)) % chips, chips)
        part, ignored = region(own_ref.shape, pieces, way, piece)
        there = all_ref.at[(owner,) + part]
        return pltpu.make_async_remote_copy(
            src_ref=own_ref.at[part] if first else there,
            dst_ref=there,
            send_sem=send_sem.at[way, piece, step],
            recv_sem=recv_sem.at[way, piece, step],
            device_id={"fsdp": right if way == 0 else left},
            device_id_type=MESH,
        )

    streams = [(way, piece) for piece in range(pieces) for way in range(2)]
    for way, piece in streams:
        copy(way, 0, piece, True).start()

    def body(step, carried):
        for way, piece in streams:
            copy(way, step - 1, piece, False).wait_recv()
            copy(way, step, piece, False).start()
        return carried

    lax.fori_loop(1, chips - 1, body, 0)
    for way, piece in streams:
        copy(way, chips - 2, piece, False).wait_recv()

    def finish(step, carried):
        for way, piece in streams:
            copy(way, step, piece, False).wait_send()
        return carried

    lax.fori_loop(0, chips - 1, finish, 0)
    keep.wait()


def ring_gather(own, chips, ident):
    rows, columns = own.shape
    pieces = 2 if rows % 64 == 0 else 1
    return pl.pallas_call(
        functools.partial(gather_kernel, chips, pieces),
        out_shape=jax.ShapeDtypeStruct((chips, rows, columns), own.dtype),
        in_specs=[pl.BlockSpec(memory_space=pl.ANY)],
        out_specs=pl.BlockSpec(memory_space=pl.ANY),
        scratch_shapes=[
            pltpu.SemaphoreType.DMA,
            pltpu.SemaphoreType.DMA((2, pieces, chips - 1)),
            pltpu.SemaphoreType.DMA((2, pieces, chips - 1)),
        ],
        compiler_params=pltpu.CompilerParams(collective_id=ident, has_side_effects=True),
        cost_estimate=cost(45),
    )(own)


def scatter_kernel(chips, pieces, parts_ref, sum_ref, held, send_sem, recv_sem):
    chip, ring, right, left = ring_places(chips)
    ring_barrier(right, left)

    def owner_of(way, step):
        shift = chips - 1 - step if way == 0 else 1 + step
        return chip_of((ring + shift) % chips, chips)

    def copy(way, step, piece, first):
        part, place = region(sum_ref.shape, pieces, way, piece)
        return pltpu.make_async_remote_copy(
            src_ref=(
                parts_ref.at[(owner_of(way, step),) + part]
                if first
                else held.at[(way, step - 1) + place]
            ),
            dst_ref=held.at[(way, step) + place],
            send_sem=send_sem.at[way, piece, step],
            recv_sem=recv_sem.at[way, piece, step],
            device_id={"fsdp": right if way == 0 else left},
            device_id_type=MESH,
        )

    streams = [(way, piece) for piece in range(pieces) for way in range(2)]
    for way, piece in streams:
        copy(way, 0, piece, True).start()

    def arrived(way, step, piece):
        copy(way, step, piece, True).wait_recv()
        part, place = region(sum_ref.shape, pieces, way, piece)
        here = parts_ref[(owner_of(way, step + 1),) + part]
        return held[(way, step) + place].astype(single) + here.astype(single)

    def body(step, carried):
        for way, piece in streams:
            total = arrived(way, step - 1, piece)
            part, place = region(sum_ref.shape, pieces, way, piece)
            held[(way, step - 1) + place] = total.astype(held.dtype)
            copy(way, step, piece, False).start()
        return carried

    lax.fori_loop(1, chips - 1, body, 0)
    for way, piece in streams:
        part, place = region(sum_ref.shape, pieces, way, piece)
        sum_ref[part] = arrived(way, chips - 2, piece)

    def finish(step, carried):
        for way, piece in streams:
            copy(way, step, piece, True).wait_send()
        return carried

    lax.fori_loop(0, chips - 1, finish, 0)


def ring_scatter(parts, chips, ident):
    rows, columns = parts.shape[1:]
    pieces = 2 if rows % 64 == 0 else 1
    return pl.pallas_call(
        functools.partial(scatter_kernel, chips, pieces),
        out_shape=jax.ShapeDtypeStruct((rows, columns), single),
        in_specs=[pl.BlockSpec(memory_space=pltpu.VMEM)],
        out_specs=pl.BlockSpec(memory_space=pltpu.VMEM),
        scratch_shapes=[
            pltpu.VMEM((2, chips - 1) + half_shape(rows, columns), parts.dtype),
            pltpu.SemaphoreType.DMA((2, pieces, chips - 1)),
            pltpu.SemaphoreType.DMA((2, pieces, chips - 1)),
        ],
        compiler_params=pltpu.CompilerParams(
            collective_id=ident, has_side_effects=True, vmem_limit_bytes=56 * 2**20
        ),
        cost_estimate=cost(45),
    )(parts)


def norm_back(values, scales, grad):
    inverse = lax.rsqrt(jnp.mean(values * values, axis=-1, keepdims=True) + eps_norm)
    bent = grad * (1.0 + scales)
    slope = jnp.mean(bent * values, axis=-1, keepdims=True) * (inverse * inverse * inverse)
    return bent * inverse - values * slope, jnp.sum(grad * values * inverse, axis=0, keepdims=True)


def gelu_parts(gate):
    root = math.sqrt(2.0 / math.pi)
    square = gate * gate
    bend = jnp.tanh(root * gate * (1.0 + 0.044715 * square))
    half = 0.5 * (1.0 + bend)
    slope = half + 0.5 * gate * (1.0 - bend * bend) * (root * (1.0 + 3.0 * 0.044715 * square))
    return gate * half, slope


def dot_nt(left, right):
    return lax.dot_general(left, right, (((1,), (1,)), ((), ())), preferred_element_type=single)


def dot_nn(left, right):
    return lax.dot_general(left, right, (((1,), (0,)), ((), ())), preferred_element_type=single)


def dot_tn(left, right):
    return lax.dot_general(left, right, (((0,), (0,)), ((), ())), preferred_element_type=single)


class Ring:
    def __init__(self, chips, pieces, rows, send_sem, recv_sem):
        self.chips, self.pieces, self.half = chips, pieces, rows // 2
        self.size = rows // 2 // pieces
        self.chip, self.ring, self.right, self.left = ring_places(chips)
        self.send_sem, self.recv_sem = send_sem, recv_sem
        self.streams = [(way, piece) for piece in range(pieces) for way in range(2)]

    def owner(self, way, step):
        shift = self.chips - step if way == 0 else step
        return chip_of((self.ring + shift) % self.chips, self.chips)

    def copy(self, source, target, way, piece, step):
        return pltpu.make_async_remote_copy(
            src_ref=source,
            dst_ref=target,
            send_sem=self.send_sem.at[way, piece, step],
            recv_sem=self.recv_sem.at[way, piece, step],
            device_id={"fsdp": self.right if way == 0 else self.left},
            device_id_type=MESH,
        )

    def part(self, way, piece):
        return pl.ds(way * self.half + piece * self.size, self.size)

    def place(self, piece):
        return pl.ds(piece * self.size, self.size)

    def gather_copy(self, all_ref, way, piece, step):
        there = all_ref.at[self.owner(way, step), self.part(way, piece)]
        return self.copy(there, there, way, piece, step)

    def of(self, only):
        return [(way, piece) for way, piece in self.streams if only is None or piece == only]

    def gather_step(self, all_ref, step, only=None):
        for way, piece in self.of(only):

            @pl.when(step > 0)
            def _():
                self.gather_copy(all_ref, way, piece, step - 1).wait_recv()

            @pl.when(step < self.chips - 1)
            def _():
                self.gather_copy(all_ref, way, piece, step).start()

    def scatter_copy(self, parts_ref, held, way, piece, step, first):
        source = (
            parts_ref.at[self.owner(way, step + 1), self.part(way, piece)]
            if first
            else held.at[way, step - 1, self.place(piece)]
        )
        return self.copy(source, held.at[way, step, self.place(piece)], way, piece, step)

    def scatter_total(self, parts_ref, held, way, piece, step):
        self.scatter_copy(parts_ref, held, way, piece, step, True).wait_recv()
        here = parts_ref[self.owner(way, step + 2), self.part(way, piece)]
        return held[way, step, self.place(piece)].astype(single) + here.astype(single)

    def scatter_step(self, parts_ref, held, step, only=None):
        for way, piece in self.of(only):

            @pl.when(step == 0)
            def _():
                self.scatter_copy(parts_ref, held, way, piece, 0, True).start()

            @pl.when(step > 0)
            def _():
                total = self.scatter_total(parts_ref, held, way, piece, step - 1)
                held[way, step - 1, self.place(piece)] = total.astype(held.dtype)
                self.scatter_copy(parts_ref, held, way, piece, step, False).start()

    def scatter_end(self, parts_ref, held, sum_ref):
        for way, piece in self.streams:
            sum_ref[self.part(way, piece)] = self.scatter_total(
                parts_ref, held, way, piece, self.chips - 2
            )

    def finish(self, example):
        def body(step, carried):
            for way, piece in self.streams:
                self.copy(example, example, way, piece, step).wait_send()
            return carried

        lax.fori_loop(0, self.chips - 1, body, 0)


def quad_peers(chips):
    side = lax.axis_index("head")
    index = lax.axis_index("fsdp")
    chip, core = index // 2, index % 2
    ring = ring_of(chip, chips)
    around = [2 * chip_of((ring + hop) % chips, chips) + core for hop in range(1, chips)]
    return side, core, {"head": 1 - side}, {"fsdp": 2 * chip + 1 - core}, around


def wide_barrier(to_side, to_core, around):
    barrier = pltpu.get_barrier_semaphore()
    for target in [to_side, to_core] + [{"fsdp": other} for other in around]:
        pl.semaphore_signal(barrier, inc=1, device_id=target, device_id_type=MESH)
    pl.semaphore_wait(barrier, 2 + len(around))


def quad_barrier(to_side, to_core, right, left):
    barrier = pltpu.get_barrier_semaphore()
    for target in (to_side, to_core, {"fsdp": right}, {"fsdp": left}):
        pl.semaphore_signal(barrier, inc=1, device_id=target, device_id_type=MESH)
    pl.semaphore_wait(barrier, 4)


def remote(source, target, send_sem, recv_sem, device):
    return pltpu.make_async_remote_copy(
        src_ref=source,
        dst_ref=target,
        send_sem=send_sem,
        recv_sem=recv_sem,
        device_id=device,
        device_id_type=MESH,
    )


class Total:
    def __init__(self, value, near, blocks, send_sem, recv_sem, peers, chip):
        self.value, self.near, self.blocks = value, near, blocks
        self.send_sem, self.recv_sem = send_sem, recv_sem
        side, core, self.to_side, self.to_core, self.around = peers
        self.chip = chip
        self.first = remote(value.at[0], near.at[0], send_sem.at[0], recv_sem.at[0], self.to_side)
        self.second = remote(value.at[1], near.at[1], send_sem.at[1], recv_sem.at[1], self.to_core)

    def spread(self, hop):
        here = self.blocks.at[self.chip]
        return remote(
            here,
            here,
            self.send_sem.at[1 + hop],
            self.recv_sem.at[1 + hop],
            {"fsdp": self.around[hop - 1]},
        )

    def start(self):
        self.first.start()

    def over_cores(self):
        self.first.wait_recv()
        self.value[1] = self.value[0] + self.near[0]
        self.second.start()

    def over_ring(self):
        self.second.wait_recv()
        self.blocks[self.chip] = self.value[1] + self.near[1]
        for hop in range(1, len(self.around) + 1):
            self.spread(hop).start()

    def end(self):
        for hop in range(1, len(self.around) + 1):
            self.spread(hop).wait_recv()
        total = self.blocks[0]
        for other in range(1, len(self.around) + 1):
            total = total + self.blocks[other]
        self.first.wait_send()
        self.second.wait_send()
        for hop in range(1, len(self.around) + 1):
            self.spread(hop).wait_send()
        return total


def total_scratch(chips, width):
    return [
        pltpu.VMEM((2, 4, width), single),
        pltpu.VMEM((2, 4, width), single),
        pltpu.VMEM((chips, 4, width), single),
        pltpu.SemaphoreType.DMA((chips + 1,)),
        pltpu.SemaphoreType.DMA((chips + 1,)),
    ]


def turn(raw, cosine, sine):
    halfway = raw.shape[1] // 2
    former, latter = raw[:, :halfway], raw[:, halfway:]
    return jnp.concatenate(
        [former * cosine - latter * sine, latter * cosine + former * sine], axis=1
    )


def front_kernel(
    chips,
    cuts,
    own_ref,
    gains_ref,
    resid_ref,
    pace_ref,
    wide_units_ref,
    rows_out,
    scales_ref,
    normed_out,
    query_ref,
    keyval_out,
    attended_ref,
    inverse_ref,
    projected_ref,
    cosine_ref,
    sine_ref,
    key_cosine_ref,
    key_sine_ref,
    own_units_ref,
    core_units_ref,
    side_units_ref,
    diag_units_ref,
    rows_ref,
    normed_ref,
    keyval_ref,
    all_rows,
    both,
    total,
    sums,
    product,
    across_put,
    across_got,
    along_put,
    along_got,
    cast_in,
    cast_out,
    value,
    near,
    blocks,
    total_send,
    total_recv,
    send_sem,
    recv_sem,
    place_sem,
    peer_sem,
    key_send,
    key_recv,
    quad_send,
    quad_recv,
    cast_sem,
    out_sem,
    bulk_send,
    bulk_recv,
):
    share, width = own_ref.shape[1:]
    tok_rows = resid_ref.shape[0]
    tokens = 4 * tok_rows
    half = width // 2
    pairs = chips // 4
    scale = 1.0 / math.sqrt(HD)
    seq_len = min(SEQ_LEN, tokens * chips)
    chip, ring, right, left = ring_places(chips)
    peers = quad_peers(chips)
    side, core, to_side, to_core, around = peers
    cast_rows = cast_in.shape[1]
    casts = wide_units_ref.shape[0] // cast_rows

    def cast_load(tile):
        rows = pl.ds(tile * cast_rows, cast_rows)
        return pltpu.make_async_copy(
            wide_units_ref.at[rows], cast_in.at[tile % 2], cast_sem.at[0, tile % 2]
        )

    def cast_store(tile):
        rows = pl.ds(tile * cast_rows, cast_rows)
        return pltpu.make_async_copy(
            cast_out.at[tile % 2], own_units_ref.at[rows], cast_sem.at[1, tile % 2]
        )

    def cast(first, last):
        for tile in range(first, last):
            cast_load(tile).wait()
            if tile >= 3:
                cast_store(tile - 2).wait()
            cast_out[tile % 2] = cast_in[tile % 2].astype(bfloat)
            cast_store(tile).start()
            if tile + 2 < casts:
                cast_load(tile + 2).start()

    outs = [
        pltpu.make_async_copy(rows_ref.at[0:2], rows_out.at[0:2], out_sem.at[0]),
        pltpu.make_async_copy(rows_ref.at[2], rows_out.at[2], out_sem.at[1]),
        pltpu.make_async_copy(normed_ref, normed_out, out_sem.at[2]),
        pltpu.make_async_copy(keyval_ref, keyval_out, out_sem.at[3]),
    ]
    def tables():
        place_in = chip * tokens + lax.broadcasted_iota(jnp.int32, cosine_ref.shape, 0)
        angles = (place_in % seq_len).astype(single) * pace_ref[...]
        cosine_ref[...] = jnp.cos(angles)
        sine_ref[...] = jnp.sin(angles)
        key_cosine_ref[...] = jnp.where(side == 0, cosine_ref[...], 1.0)
        key_sine_ref[...] = jnp.where(side == 0, sine_ref[...], 0.0)

    cast_load(0).start()
    cast_load(1).start()
    all_rows[chip] = own_ref[...].astype(bfloat)
    value[0] = gains_ref[...].astype(bfloat).astype(single)
    wide_barrier(to_side, to_core, around)
    gains_total = Total(value, near, blocks, total_send, total_recv, peers, chip)
    gains_total.start()
    streams = [(way, slot) for slot in range(2) for way in range(2)]
    out_streams = [(way, 2) for way in range(2)]
    key_streams = [(way, kind) for kind in range(2) for way in range(2)]

    def owner_of(way, step):
        return chip_of((ring + (chips - step if way == 0 else step)) % chips, chips)

    def hop(way, slot, step):
        there = all_rows.at[owner_of(way, step), slot, :, pl.ds(way * half, half)]
        return remote(
            there,
            there,
            send_sem.at[way, slot, step],
            recv_sem.at[way, slot, step],
            {"fsdp": right if way == 0 else left},
        )

    def key_hop(way, kind, step):
        there = keyval_ref.at[owner_of(way, step), kind, pl.ds(way * (tokens // 2), tokens // 2)]
        return remote(
            there,
            there,
            key_send.at[way, kind, step],
            key_recv.at[way, kind, step],
            {"fsdp": right if way == 0 else left},
        )

    def goal(way, slot, step):
        owner = owner_of(way, step)
        deep = owner // pairs
        unit = (owner % pairs) * 2 + core
        taker, head = (deep % 2, deep // 2) if slot == 1 else (deep // 2, deep % 2)
        columns = pl.ds(way * half, half)
        source = all_rows.at[owner, slot, :, columns]
        start = pl.multiple_of(head * HD + unit * share, share)
        target = rows_ref.at[slot, pl.ds(start, share), columns]
        sem = place_sem.at[way, slot, step]

        def here():
            return pltpu.make_async_copy(source, target, sem)

        def there():
            return remote(source, target, sem, peer_sem.at[way, slot, step], to_core)

        return taker, here, there

    def place(way, slot, step):
        taker, here, there = goal(way, slot, step)

        @pl.when(taker == core)
        def _():
            here().start()

        @pl.when(taker != core)
        def _():
            there().start()

    def placed(way, slot, step):
        taker, here, there = goal(way, slot, step)

        @pl.when(taker == core)
        def _():
            here().wait()
            there().wait_recv()

        @pl.when(taker != core)
        def _():
            there().wait_send()

    def pass_on(which, step):
        for way, slot in which:

            @pl.when(step > 0)
            def _():
                hop(way, slot, step - 1).wait_recv()

            @pl.when(step < chips - 1)
            def _():
                hop(way, slot, step).start()

            place(way, slot, step)

    def settle(which):
        def body(step, carried):
            for way, slot in which:
                placed(way, slot, step)

                @pl.when(step < chips - 1)
                def _():
                    hop(way, slot, step).wait_send()

            return carried

        lax.fori_loop(0, chips, body, 0)

    def quad_copy(source, target, index, device):
        return remote(source, target, quad_send.at[index], quad_recv.at[index], device)

    mine = normed_ref.at[core, side]
    along = quad_copy(mine, mine, 0, to_side)
    across = quad_copy(normed_ref.at[core], normed_ref.at[core], 1, to_core)

    def bulk_side(part):
        rows = pl.ds(cuts[part], cuts[part + 1] - cuts[part])
        return remote(
            own_units_ref.at[rows],
            side_units_ref.at[rows],
            bulk_send.at[part],
            bulk_recv.at[part],
            to_side,
        )

    def bulk_diag(part):
        rows = pl.ds(cuts[part], cuts[part + 1] - cuts[part])
        return remote(
            side_units_ref.at[rows],
            diag_units_ref.at[rows],
            bulk_send.at[3 + part],
            bulk_recv.at[3 + part],
            to_core,
        )

    bulk_core = remote(own_units_ref, core_units_ref, bulk_send.at[6], bulk_recv.at[6], to_core)
    for way, slot in streams:
        hop(way, slot, 0).start()
    cast(0, 1)
    cast_store(0).wait()
    bulk_side(0).start()
    gains_total.over_cores()
    for way, slot in streams:
        place(way, slot, 0)
    gains_total.over_ring()
    pass_on(streams, 1)
    cast(1, 3)
    tables()
    pass_on(streams, 2)
    scales_ref[...] = gains_total.end()
    normed_ref[core, side] = norm_scale(resid_ref[...], scales_ref[0:1]).astype(bfloat)
    along.start()
    cast(3, 4)
    pass_on(streams, 3)
    cast(4, 6)
    pass_on(streams, 4)
    cast(6, casts)
    cast_store(casts - 2).wait()
    cast_store(casts - 1).wait()
    bulk_core.start()
    along.wait()
    across.start()
    bulk_side(1).start()

    def body(step, carried):
        pass_on(streams, step)
        return carried

    lax.fori_loop(5, chips, body, 0)
    pass_on(out_streams, 0)
    across.wait()
    outs[2].start()
    settle(streams)
    outs[0].start()

    def project(slot, head):
        rows = slice(head * HD, head * HD + HD)
        return dot_nt(normed_ref[...].reshape(tokens, width), rows_ref[slot, rows])

    for head in range(2):
        raw = project(1, head)
        both[head] = turn(raw, key_cosine_ref[...], key_sine_ref[...]).astype(bfloat)
    swap = quad_copy(both.at[1 - side], keyval_ref.at[chip, side], 2, to_side)
    swap.start()
    bulk_side(2).start()
    for part in range(2):
        bulk_side(part).wait_recv()
        bulk_diag(part).start()
    pass_on(out_streams, 1)
    keyval_ref[chip, side] = both[side]
    for head in range(2):
        raw = project(0, head)
        query_ref[head] = turn(raw, cosine_ref[...], sine_ref[...]).astype(bfloat)
        pass_on(out_streams, 2 + head)
    total[...] = jnp.zeros_like(total)
    sums[...] = jnp.zeros_like(sums)
    swap.wait()

    def block(way, owner):
        part = tokens // 2
        key = keyval_ref[owner, 0, way * part : way * part + part]
        val = keyval_ref[owner, 1, way * part : way * part + part]
        row = lax.broadcasted_iota(jnp.int32, (tokens, part), 0)
        column = lax.broadcasted_iota(jnp.int32, (tokens, part), 1)
        allowed = row + (chip - owner) * tokens - way * part >= column

        def one_head(head, carried):
            bent = jnp.tanh(dot_nt(query_ref[head], key) * (scale / softcap))
            powers = jnp.where(allowed, jnp.exp(softcap * bent), 0.0)
            sums[head] += powers[:, : part // 2] + powers[:, part // 2 :]
            total[head] += dot_nn(powers.astype(bfloat), val)
            return carried

        for head in range(2):
            one_head(head, 0)

    def key_body(step, carried):
        for way, kind in key_streams:

            @pl.when(step > 0)
            def _():
                key_hop(way, kind, step - 1).wait_recv()

            @pl.when(step < chips - 1)
            def _():
                key_hop(way, kind, step).start()

        for way in range(2):
            owner = owner_of(way, step)

            @pl.when(owner <= chip)
            def _():
                block(way, owner)

            if way == 0:

                @pl.when(step < chips - 4)
                def _():
                    pass_on(out_streams, step + 4)

        return carried

    lax.fori_loop(0, chips, key_body, 0)
    outs[3].start()
    bulk_side(2).wait_recv()
    bulk_diag(2).start()
    settle(out_streams)
    outs[1].start()
    for head in range(2):
        inverse = 1.0 / jnp.sum(sums[head], axis=-1, keepdims=True)
        inverse_ref[head] = jnp.broadcast_to(inverse, inverse_ref.shape[1:])
        attended_ref[:, head * HD : head * HD + HD] = (total[head] * inverse).astype(bfloat)
    span = width // 3
    tiles = [slice(tile * span, tile * span + span) for tile in range(3)]

    def project_out(part, ref, columns):
        first = pl.ds(pl.multiple_of(part * 2 * tok_rows, 2 * tok_rows), 2 * tok_rows)
        made = dot_nn(attended_ref[first], rows_ref[2, :, columns])
        ref[:, :, columns] = made.reshape(2, tok_rows, span).astype(ref.dtype)

    across = [
        quad_copy(across_put.at[:, :, columns], across_got.at[:, :, columns], 3 + tile, to_core)
        for tile, columns in enumerate(tiles)
    ]
    along = [
        quad_copy(along_put.at[:, columns], along_got.at[:, columns], 6 + tile, to_side)
        for tile, columns in enumerate(tiles)
    ]
    for tile, columns in enumerate(tiles):
        project_out(1 - core, across_put, columns)
        across[tile].start()
    for tile, columns in enumerate(tiles):
        project_out(core, product, columns)
        across[tile].wait()
        given = product[1 - side, :, columns] + across_got[1 - side, :, columns].astype(single)
        along_put[:, columns] = given.astype(bfloat)
        along[tile].start()

    def key_settle(step, carried):
        for way, kind in key_streams:
            key_hop(way, kind, step).wait_send()
        return carried

    lax.fori_loop(0, chips - 1, key_settle, 0)
    for out in outs:
        out.wait()
    bulk_core.wait()
    for part in range(3):
        bulk_side(part).wait_send()
        bulk_diag(part).wait()
    for tile, columns in enumerate(tiles):
        along[tile].wait()
        kept = product[side, :, columns] + across_got[side, :, columns].astype(single)
        projected_ref[:, columns] = kept + along_got[:, columns].astype(single)


def cost(micros):
    return pl.CostEstimate(flops=int(micros * 1e9), bytes_accessed=0, transcendentals=0)


def front(attn_weight, gains, resid_in, pace, ffn_wide, chips, ident):
    share, width = attn_weight.shape[1:]
    tok_rows = resid_in.shape[0]
    tokens = 4 * tok_rows
    units = ffn_wide.shape[0]
    cuts = (0, units // 9, units // 3, 2 * units // 3)
    vmem = pl.BlockSpec(memory_space=pltpu.VMEM)
    anywhere = pl.BlockSpec(memory_space=pl.ANY)
    return pl.pallas_call(
        functools.partial(front_kernel, chips, cuts),
        out_shape=(
            jax.ShapeDtypeStruct((3, 2 * HD, width), bfloat),
            jax.ShapeDtypeStruct((4, width), single),
            jax.ShapeDtypeStruct((2, 2, tok_rows, width), bfloat),
            jax.ShapeDtypeStruct((2, tokens, HD), bfloat),
            jax.ShapeDtypeStruct((chips, 2, tokens, HD), bfloat),
            jax.ShapeDtypeStruct((tokens, 2 * HD), bfloat),
            jax.ShapeDtypeStruct((2, tokens, 128), single),
            jax.ShapeDtypeStruct((tok_rows, width), single),
        )
        + (jax.ShapeDtypeStruct((tokens, HD // 2), single),) * 4
        + (jax.ShapeDtypeStruct((units, width), bfloat),) * 2
        + (jax.ShapeDtypeStruct((2 * units // 3, width), bfloat),) * 2,
        in_specs=[vmem] * 4 + [anywhere],
        out_specs=(anywhere, vmem, anywhere, vmem, anywhere, vmem, vmem, vmem)
        + (vmem,) * 4
        + (anywhere,) * 4,
        scratch_shapes=[
            pltpu.VMEM((3, 2 * HD, width), bfloat),
            pltpu.VMEM((2, 2, tok_rows, width), bfloat),
            pltpu.VMEM((chips, 2, tokens, HD), bfloat),
            pltpu.VMEM((chips, 3, share, width), bfloat),
            pltpu.VMEM((2, tokens, HD), bfloat),
            pltpu.VMEM((2, tokens, HD), single),
            pltpu.VMEM((2, tokens, 128), single),
            pltpu.VMEM((2, tok_rows, width), single),
            pltpu.VMEM((2, tok_rows, width), bfloat),
            pltpu.VMEM((2, tok_rows, width), bfloat),
            pltpu.VMEM((tok_rows, width), bfloat),
            pltpu.VMEM((tok_rows, width), bfloat),
            pltpu.VMEM((2, units // 9, width), single),
            pltpu.VMEM((2, units // 9, width), bfloat),
        ]
        + total_scratch(chips, width)
        + [
            pltpu.SemaphoreType.DMA((2, 3, chips - 1)),
            pltpu.SemaphoreType.DMA((2, 3, chips - 1)),
            pltpu.SemaphoreType.DMA((2, 3, chips)),
            pltpu.SemaphoreType.DMA((2, 3, chips)),
            pltpu.SemaphoreType.DMA((2, 2, chips - 1)),
            pltpu.SemaphoreType.DMA((2, 2, chips - 1)),
            pltpu.SemaphoreType.DMA((9,)),
            pltpu.SemaphoreType.DMA((9,)),
            pltpu.SemaphoreType.DMA((2, 2)),
            pltpu.SemaphoreType.DMA((4,)),
            pltpu.SemaphoreType.DMA((7,)),
            pltpu.SemaphoreType.DMA((7,)),
        ],
        compiler_params=pltpu.CompilerParams(
            collective_id=ident, has_side_effects=True, vmem_limit_bytes=60 * 2**20
        ),
        cost_estimate=cost(140),
    )(attn_weight, gains, resid_in, pace, ffn_wide)


def tail_kernel(
    chips,
    d_proj_ref,
    query_ref,
    keyval_in,
    attended_ref,
    inverse_ref,
    rows_in,
    normed_in,
    cosine_ref,
    sine_ref,
    key_cosine_ref,
    key_sine_ref,
    resid_ref,
    d_mid_ref,
    scales_ref,
    gains_ref,
    units_own_ref,
    units_other_ref,
    sum_ref,
    tokens_ref,
    total_ref,
    units_ref,
    units_got_ref,
    units_mine_ref,
    keyval_ref,
    rows_ref,
    normed_ref,
    d_all,
    d_out,
    delta,
    d_query,
    d_block,
    first_put,
    held_keys,
    swapped,
    d_raw,
    out_rows,
    parts,
    out_parts,
    held,
    out_held,
    across_got,
    along_put,
    along_got,
    value,
    near,
    blocks,
    total_send,
    total_recv,
    key_send,
    key_recv,
    place_sem,
    peer_sem,
    send_sem,
    recv_sem,
    out_send,
    out_recv,
    quad_send,
    quad_recv,
    load_sem,
    bulk_send,
    bulk_recv,
):
    tokens = query_ref.shape[1]
    half = tokens // 2
    width = resid_ref.shape[1]
    share = out_parts.shape[1]
    pairs = chips // 4
    scale = 1.0 / math.sqrt(HD)
    peers = quad_peers(chips)
    side, core, to_side, to_core, around = peers
    rings = [Ring(chips, 1, share, send_sem.at[slot], recv_sem.at[slot]) for slot in range(2)]
    ring = rings[0]
    out_ring = Ring(chips, 1, share, out_send, out_recv)
    chip = ring.chip
    gains_total = Total(value, near, blocks, total_send, total_recv, peers, chip)
    arrays = [
        pltpu.make_async_copy(rows_in.at[2], rows_ref.at[2], load_sem.at[3]),
        pltpu.make_async_copy(keyval_in, keyval_ref, load_sem.at[4]),
        pltpu.make_async_copy(normed_in, normed_ref, load_sem.at[5]),
        pltpu.make_async_copy(rows_in.at[0:2], rows_ref.at[0:2], load_sem.at[6]),
    ]
    d_all[core, side] = d_proj_ref[...]
    wide_barrier(to_side, to_core, around)

    def quad_copy(source, target, index, device):
        return remote(source, target, quad_send.at[index], quad_recv.at[index], device)

    def bulk(kind):
        return remote(
            units_ref.at[pl.ds(kind * (units_ref.shape[0] // 3), units_ref.shape[0] // 3)],
            units_got_ref.at[pl.ds(kind * (units_ref.shape[0] // 3), units_ref.shape[0] // 3)],
            bulk_send.at[kind],
            bulk_recv.at[kind],
            to_side,
        )

    units = units_ref.shape[0]
    ours = out_rows.reshape(6 * HD, width).at[pl.ds(0, units)]
    theirs = parts.reshape(2 * chips * share, width).at[pl.ds(0, units)]
    loads = (
        pltpu.make_async_copy(units_own_ref.at[1], ours, load_sem.at[0]),
        pltpu.make_async_copy(units_other_ref.at[1], theirs, load_sem.at[1]),
    )
    store = pltpu.make_async_copy(ours, units_ref, load_sem.at[2])
    spare = held.reshape(2 * (chips - 1) * share, width).at[pl.ds(0, units)]
    mine_loads = (
        pltpu.make_async_copy(units_own_ref.at[0], ours, load_sem.at[7]),
        pltpu.make_async_copy(units_other_ref.at[0], spare, load_sem.at[8]),
    )
    mine_store = pltpu.make_async_copy(ours, units_mine_ref, load_sem.at[9])
    mine_loads[1].start()

    def add_up(more):
        for kind in range(3):
            rows = slice(kind * units // 3, (kind + 1) * units // 3)
            ours[rows] = (ours[rows].astype(single) + more[rows].astype(single)).astype(bfloat)
    for load in loads:
        load.start()
    for array in arrays:
        array.start()
    quarter = tokens // 8
    halves = [slice(part * quarter, part * quarter + quarter) for part in range(2)]
    along = [
        quad_copy(d_all.at[core, side, rows], d_all.at[core, side, rows], part, to_side)
        for part, rows in enumerate(halves)
    ]
    across = quad_copy(d_all.at[core, side], d_all.at[core, side], 2, to_core)
    relay = [
        quad_copy(d_all.at[core, 1 - side, rows], d_all.at[core, 1 - side, rows], 3 + part, to_core)
        for part, rows in enumerate(halves)
    ]
    for part in range(2):
        along[part].start()
    across.start()
    d_query[...] = jnp.zeros_like(d_query)
    for load in loads:
        load.wait()
    add_up(theirs)
    store.start()
    for part in range(2):
        along[part].wait()
        relay[part].start()
    store.wait()
    bulk(0).start()
    bulk(1).start()
    mine_loads[0].start()
    across.wait()
    for load in mine_loads:
        load.wait()
    add_up(spare)
    mine_store.start()
    for part in range(2):
        relay[part].wait()
    for array in arrays:
        array.wait()
    d_rows = d_all[...].reshape(tokens, width)
    for head in range(2):
        columns = slice(head * HD, head * HD + HD)
        made = dot_nt(d_rows, rows_ref[2, columns]).astype(bfloat)
        d_out[head] = made
        row_dot = jnp.sum(
            made.astype(single) * attended_ref[:, columns].astype(single), axis=-1, keepdims=True
        )
        delta[head] = jnp.broadcast_to(row_dot, delta.shape[1:])

    def place(slot, head, start):
        deep = 2 * head + core if slot == 1 else 2 * core + head
        for unit in range(4):
            source = out_rows.at[slot, head, pl.ds(unit * share, share)]
            owner = deep * pairs + unit // 2
            target = out_parts.at[owner] if slot == 2 else parts.at[slot, owner]
            sem = place_sem.at[slot, head, unit]

            def here():
                return pltpu.make_async_copy(source, target, sem)

            def there():
                return remote(source, target, sem, peer_sem.at[slot, head, unit], to_core)

            @pl.when(core == unit % 2)
            def _():
                if start:
                    here().start()
                else:
                    here().wait()
                    there().wait_recv()

            @pl.when(core != unit % 2)
            def _():
                if start:
                    there().start()
                else:
                    there().wait_send()

    def term(slot, head, left, right):
        out_rows[slot, head] = dot_tn(left, right).astype(bfloat)
        place(slot, head, True)

    def block(way, owner):
        key = keyval_ref[owner, 0, way * half : way * half + half]
        val = keyval_ref[owner, 1, way * half : way * half + half]
        row = lax.broadcasted_iota(jnp.int32, (tokens, half), 0)
        column = lax.broadcasted_iota(jnp.int32, (tokens, half), 1)
        allowed = row + (chip - owner) * tokens - way * half >= column

        def one_head(head, carried):
            bent = jnp.tanh(dot_nt(query_ref[head], key) * (scale / softcap))
            inverse = jnp.concatenate([inverse_ref[head]] * (half // 128), axis=1)
            row_dot = jnp.concatenate([delta[head]] * (half // 128), axis=1)
            probs = jnp.where(allowed, jnp.exp(softcap * bent), 0.0) * inverse
            d_probs = dot_nt(d_out[head], val)
            d_scores = (probs * (d_probs - row_dot) * (1.0 - bent * bent)).astype(bfloat)
            d_block[way, 0] += dot_tn(d_scores, query_ref[head]) * scale
            d_block[way, 1] += dot_tn(probs.astype(bfloat), d_out[head])
            d_query[head] += dot_nn(d_scores, key)
            return carried

        for head in range(2):
            one_head(head, 0)

    def key_copy(way, kind, step, first):
        return remote(
            first_put.at[way, kind] if first else held_keys.at[way, step - 1, kind],
            held_keys.at[way, step, kind],
            key_send.at[way, kind, step],
            key_recv.at[way, kind, step],
            {"fsdp": ring.right if way == 0 else ring.left},
        )

    streams = [(way, kind) for kind in range(2) for way in range(2)]

    early = 3

    def key_blocks(step):
        for way in range(2):
            owner = ring.owner(way, step + 1)
            d_block[way] = jnp.zeros(d_block.shape[1:], single)
            if way == 1:

                @pl.when((step >= early) & (step < chips - 1))
                def _():
                    out_ring.scatter_step(out_parts, out_held, step - early)

            @pl.when(owner <= chip)
            def _():
                block(way, owner)

    def key_body(step, carried):
        key_blocks(step)
        for way, kind in streams:

            @pl.when(step == 0)
            def _():
                first_put[way, kind] = d_block[way, kind].astype(bfloat)
                key_copy(way, kind, 0, True).start()

            @pl.when(step > 0)
            def _():
                key_copy(way, kind, step - 1, True).wait_recv()
                summed = held_keys[way, step - 1, kind].astype(single) + d_block[way, kind]
                held_keys[way, step - 1, kind] = summed.astype(bfloat)
                key_copy(way, kind, step, False).start()

        @pl.when(step == 0)
        def _():
            for head in range(2):
                left = attended_ref[:, head * HD : head * HD + HD]
                term(2, head, left, d_all[...].reshape(tokens, width))

        @pl.when(step == early - 1)
        def _():
            key_blocks(chips - 1)
            for way in range(2):
                for kind in range(2):
                    rows = slice(way * half, way * half + half)
                    swapped[2 + kind, rows] = d_block[way, kind].astype(bfloat)
            for head in range(2):
                place(2, head, False)

        return carried

    lax.fori_loop(0, chips - 1, key_body, 0)
    mine_store.wait()

    normed = normed_ref[...].reshape(tokens, width)
    for way in range(2):
        rows = slice(way * half, way * half + half)
        for kind in range(2):
            key_copy(way, kind, chips - 2, True).wait_recv()
            summed = held_keys[way, chips - 2, kind].astype(single)
            summed = summed + swapped[2 + kind, rows].astype(single)
            swapped[2 + kind, rows] = summed.astype(bfloat)
    swap = quad_copy(swapped.at[3 - side], swapped.at[side], 5, to_side)
    swap.start()
    out_ring.scatter_step(out_parts, out_held, chips - 4)
    for head in range(2):
        turned = turn(d_query[head] * scale, cosine_ref[...], -sine_ref[...])
        d_raw[head] = turned.astype(bfloat)
        term(0, head, d_raw[head], normed)
    out_ring.scatter_step(out_parts, out_held, chips - 3)
    for head in range(2):
        place(0, head, False)
    rings[0].scatter_step(parts.at[0], held.at[0], 0)
    swap.wait()
    bulk(2).start()
    swapped[side] = swapped[2 + side]
    for head in range(2):
        turned = turn(swapped[head].astype(single), key_cosine_ref[...], -key_sine_ref[...])
        d_raw[2 + head] = turned.astype(bfloat)
        term(1, head, d_raw[2 + head], normed)
    out_ring.scatter_step(out_parts, out_held, chips - 2)
    rings[0].scatter_step(parts.at[0], held.at[0], 1)
    span = width // 3

    def d_input(tile, carried):
        columns = pl.ds(pl.multiple_of(tile * span, span), span)
        made = dot_nn(d_raw[0], rows_ref[0, 0:HD, columns])
        made = made + dot_nn(d_raw[1], rows_ref[0, HD:, columns])
        made = made + dot_nn(d_raw[2], rows_ref[1, 0:HD, columns])
        made = made + dot_nn(d_raw[3], rows_ref[1, HD:, columns])
        out_rows[0, :, :, columns] = made.reshape(2, half, span).astype(bfloat)
        return carried

    for head in range(2):
        place(1, head, False)
    rings[1].scatter_step(parts.at[1], held.at[1], 0)
    lax.fori_loop(0, 3, d_input, 0)
    across = quad_copy(out_rows.at[0, 1 - core], across_got, 6, to_core)
    mine = pl.ds(pl.multiple_of(side * (half // 2), half // 2), half // 2)
    other = pl.ds(pl.multiple_of((1 - side) * (half // 2), half // 2), half // 2)
    along = quad_copy(along_put, along_got, 7, to_side)
    across.start()

    def body(step, carried):
        rings[1].scatter_step(parts.at[1], held.at[1], step)

        @pl.when(step < chips - 2)
        def _():
            rings[0].scatter_step(parts.at[0], held.at[0], step + 1)

        @pl.when(step == 1)
        def _():
            across.wait()
            given = out_rows[0, core, other].astype(single) + across_got[other].astype(single)
            along_put[...] = given.astype(bfloat)
            along.start()
            tokens_ref[...] = out_rows[0, core, mine].astype(single) + across_got[mine].astype(single)

        @pl.when(step == 4)
        def _():
            along.wait()
            tokens_ref[...] = tokens_ref[...] + along_got[...].astype(single)
            d_norm, d_gain = norm_back(resid_ref[...], scales_ref[0:1], tokens_ref[...])
            tokens_ref[...] = d_mid_ref[...] + d_norm
            value[0] = gains_ref[...]
            value[0, 0:1] = d_gain
            gains_total.start()

        @pl.when(step == 5)
        def _():
            gains_total.over_cores()

        @pl.when(step == 6)
        def _():
            gains_total.over_ring()

        return carried

    lax.fori_loop(1, chips - 1, body, 0)
    total_ref[...] = gains_total.end()
    out_ring.scatter_end(out_parts, out_held, sum_ref.at[pl.ds(2 * share, share)])
    for slot in range(2):
        rows = pl.ds(slot * share, share)
        rings[slot].scatter_end(parts.at[slot], held.at[slot], sum_ref.at[rows])
        rings[slot].finish(out_held.at[0, 0, 0 : ring.size])
    out_ring.finish(out_held.at[0, 0, 0 : out_ring.size])

    def settle(step, carried):
        for way, kind in streams:
            key_copy(way, kind, step, True).wait_send()
        return carried

    lax.fori_loop(0, chips - 1, settle, 0)
    for kind in range(3):
        bulk(kind).wait()


def tail(
    d_proj, query, keyval, attended, inverse, rows, normed, turns, locals_, own, other, chips, ident
):
    tokens = query.shape[1]
    tok_rows = tokens // 4
    width = rows.shape[2]
    share = tokens // 8
    half = tokens // 2
    vmem = pl.BlockSpec(memory_space=pltpu.VMEM)
    anywhere = pl.BlockSpec(memory_space=pl.ANY)
    return pl.pallas_call(
        functools.partial(tail_kernel, chips),
        out_shape=(
            jax.ShapeDtypeStruct((3 * share, width), single),
            jax.ShapeDtypeStruct((tok_rows, width), single),
            jax.ShapeDtypeStruct((4, width), single),
            jax.ShapeDtypeStruct(own.shape[1:], bfloat),
            jax.ShapeDtypeStruct(own.shape[1:], bfloat),
            jax.ShapeDtypeStruct(own.shape[1:], bfloat),
        ),
        in_specs=[vmem] * 2
        + [anywhere, vmem, vmem, anywhere, anywhere]
        + [vmem] * 8
        + [anywhere] * 2,
        out_specs=(vmem,) * 3 + (anywhere,) * 3,
        scratch_shapes=[
            pltpu.VMEM(keyval.shape, bfloat),
            pltpu.VMEM(rows.shape, bfloat),
            pltpu.VMEM(normed.shape, bfloat),
            pltpu.VMEM((2, 2, tok_rows, width), bfloat),
            pltpu.VMEM((2, tokens, HD), bfloat),
            pltpu.VMEM((2, tokens, 128), single),
            pltpu.VMEM((2, tokens, HD), single),
            pltpu.VMEM((2, 2, half, HD), single),
            pltpu.VMEM((2, 2, half, HD), bfloat),
            pltpu.VMEM((2, chips - 1, 2, half, HD), bfloat),
            pltpu.VMEM((4, tokens, HD), bfloat),
            pltpu.VMEM((4, tokens, HD), bfloat),
            pltpu.VMEM((3, 2, HD, width), bfloat),
            pltpu.VMEM((2, chips, share, width), bfloat),
            pltpu.VMEM((chips, share, width), bfloat),
            pltpu.VMEM((2, 2, chips - 1, share // 2, width), bfloat),
            pltpu.VMEM((2, chips - 1, share // 2, width), bfloat),
            pltpu.VMEM((2 * tok_rows, width), bfloat),
            pltpu.VMEM((tok_rows, width), bfloat),
            pltpu.VMEM((tok_rows, width), bfloat),
        ]
        + total_scratch(chips, width)
        + [
            pltpu.SemaphoreType.DMA((2, 2, chips - 1)),
            pltpu.SemaphoreType.DMA((2, 2, chips - 1)),
            pltpu.SemaphoreType.DMA((3, 2, 4)),
            pltpu.SemaphoreType.DMA((3, 2, 4)),
            pltpu.SemaphoreType.DMA((2, 2, 1, chips - 1)),
            pltpu.SemaphoreType.DMA((2, 2, 1, chips - 1)),
            pltpu.SemaphoreType.DMA((2, 1, chips - 1)),
            pltpu.SemaphoreType.DMA((2, 1, chips - 1)),
            pltpu.SemaphoreType.DMA((8,)),
            pltpu.SemaphoreType.DMA((8,)),
            pltpu.SemaphoreType.DMA((10,)),
            pltpu.SemaphoreType.DMA((3,)),
            pltpu.SemaphoreType.DMA((3,)),
        ],
        compiler_params=pltpu.CompilerParams(
            collective_id=ident, has_side_effects=True, vmem_limit_bytes=63 * 2**20
        ),
        cost_estimate=cost(160),
    )(d_proj, query, keyval, attended, inverse, rows, normed, *turns, *locals_, own, other)


def feed_kernel(
    chips,
    pieces,
    resid_ref,
    projected_ref,
    dy_ref,
    scales_ref,
    own_ref,
    side_ref,
    core_ref,
    diag_ref,
    result_ref,
    d_mid_ref,
    d_projected_ref,
    d_gains_ref,
    terms_ref,
    other_ref,
    weights,
    x_all,
    y_all,
    mid,
    both,
    hidden,
    part,
    held,
    chunk,
    wide,
    stage,
    load_sem,
    bulk_send,
    bulk_recv,
    stage_sem,
    other_sem,
    send_sem,
    recv_sem,
):
    tok_rows, width = resid_ref.shape
    units = own_ref.shape[0] // 3
    whole = 4 * units
    half = tok_rows // 2
    rings = [
        Ring(chips, pieces, tok_rows, send_sem.at[phase], recv_sem.at[phase]) for phase in range(4)
    ]
    chip = rings[0].chip
    loads = []
    for slot, ref in enumerate((own_ref, side_ref, core_ref, diag_ref)):
        for kind in range(3 if slot % 2 == 0 else 2):
            loads.append(
                pltpu.make_async_copy(
                    ref.at[pl.ds(kind * units, units)],
                    weights.at[pl.ds(kind * whole + slot * units, units)],
                    load_sem.at[slot, kind],
                )
            )
    for load in loads:
        load.start()
    mid[...] = resid_ref[...] + norm_scale(projected_ref[...], scales_ref[1:2])
    x_all[chip] = norm_scale(mid[...], scales_ref[2:3]).astype(bfloat)
    core = lax.axis_index("fsdp") % 2
    to_core = {"fsdp": 2 * chip + 1 - core}
    to_side = {"head": 1 - lax.axis_index("head")}
    quad_barrier(to_side, to_core, rings[0].right, rings[0].left)
    down_rows = [pl.ds(2 * whole + slot * units, units) for slot in range(4)]
    bulk_side = remote(
        own_ref.at[pl.ds(2 * units, units)],
        weights.at[down_rows[1]],
        bulk_send.at[0],
        bulk_recv.at[0],
        to_side,
    )
    bulk_diag = remote(
        weights.at[down_rows[1]],
        weights.at[down_rows[3]],
        bulk_send.at[1],
        bulk_recv.at[1],
        to_core,
    )
    bulk_side.start()
    span = width // 3

    def segments(pair):
        for hop in range(2):
            for way in range(2):
                start = hop * tok_rows + way * half
                owner = rings[0].owner(way, 2 * pair + hop)
                yield owner, pl.ds(way * half, half), pl.ds(start, half)

    def fetch(all_ref, pair):
        for owner, rows, here in segments(pair):
            chunk[here] = all_ref[owner, rows]

    def put(ref, pair, columns, value):
        for owner, rows, here in segments(pair):
            ref[owner, rows, columns] = value[here.start : here.start + half].astype(ref.dtype)

    def take(ref, pair, columns):
        return jnp.concatenate(
            [ref[owner, rows, columns] for owner, rows, here in segments(pair)], axis=0
        )

    def polls(ring, all_ref, pair):
        def poll(index):
            @pl.when(2 * pair + 2 < chips)
            def _():
                ring.gather_step(all_ref, 2 * pair + 2 + index // 2, index % 2)

        return poll

    def down(pair):
        chunk[:, 0:whole] = take(hidden, pair, slice(None))

        def columns_of(tile, carried):
            columns = pl.ds(pl.multiple_of(tile * span, span), span)
            put(part, pair, columns, dot_nn(chunk[:, 0:whole], weights[2 * whole :, columns]))
            return carried

        lax.fori_loop(0, 3, columns_of, 0)

    def gate_up(tile):
        rows = slice(tile * span, tile * span + span)
        wide[:, rows] = dot_nt(chunk[...], weights[rows])

    def unit(pair):
        put(both, pair, slice(None), wide[...])
        value, slope = gelu_parts(wide[:, 0:whole])
        put(hidden, pair, slice(None), value * wide[:, whole:])

    last = chips // 2 - 1

    def forward(pair, carried):
        poll = polls(rings[0], x_all, pair)
        fetch(x_all, pair)
        for tile in range(3):
            gate_up(tile)
            poll(tile)
        unit(pair)

        @pl.when(pair == last - 1)
        def _():
            bulk_side.wait_recv()
            bulk_diag.start()
            bulk_diag.wait_recv()
            down(0)

        poll(3)
        return carried

    for step in range(2):
        for piece in range(pieces):
            rings[0].gather_step(x_all, step, piece)
        if step == 0:
            for load in loads:
                load.wait()
    lax.fori_loop(0, last, forward, 0)
    rings[1].scatter_step(part, held, 0)
    down(1)
    fetch(x_all, last)
    gate_up(0)
    rings[1].scatter_step(part, held, 1)
    gate_up(1)
    gate_up(2)
    unit(last)

    def spread(step, carried):
        rings[1].scatter_step(part, held, step, 0)

        @pl.when((step % 2 == 0) & (step < chips - 2))
        def _():
            down(step // 2 + 1)

        rings[1].scatter_step(part, held, step, 1)
        return carried

    lax.fori_loop(2, chips - 1, spread, 0)
    ours = pl.ds(0, tok_rows)
    rings[1].scatter_end(part, held, wide)
    result_ref[...] = mid[...] + norm_scale(wide[ours], scales_ref[3:4])
    d_ffn, d_gain = norm_back(wide[ours], scales_ref[3:4], dy_ref[...])
    d_gains_ref[0:1] = jnp.zeros_like(d_gain)
    d_gains_ref[3:4] = d_gain
    y_all[chip] = d_ffn.astype(bfloat)
    rings[0].finish(x_all.at[0, 0 : rings[0].size])
    rings[1].finish(x_all.at[0, 0 : rings[0].size])
    bulk_side.wait_send()
    bulk_diag.wait_send()

    def d_input(pair):
        chunk[...] = take(both, pair, slice(None))

        def columns_of(tile, carried):
            columns = pl.ds(pl.multiple_of(tile * span, span), span)
            put(part, pair, columns, dot_nn(chunk[...], weights[0 : 2 * whole, columns]))
            return carried

        lax.fori_loop(0, 3, columns_of, 0)

    third = whole // 3

    def d_units(pair, tile):
        columns = slice(tile * third, tile * third + third)
        ups = slice(whole + tile * third, whole + tile * third + third)
        for owner, rows, here in segments(pair):
            value, slope = gelu_parts(both[owner, rows, columns].astype(single))
            upper = both[owner, rows, ups].astype(single)
            d_hidden = wide[here, columns]
            both[owner, rows, columns] = (d_hidden * upper * slope).astype(bfloat)
            both[owner, rows, ups] = (d_hidden * value).astype(bfloat)

    def d_hidden(first, end):
        wide[:, first:end] = dot_nt(chunk[...], weights[2 * whole + first : 2 * whole + end])

    def backward(pair, carried):
        poll = polls(rings[2], y_all, pair)
        fetch(y_all, pair)
        d_hidden(0, 2 * third)
        poll(0)
        d_hidden(2 * third, whole)
        d_units(pair, 0)
        poll(1)
        d_units(pair, 1)
        d_units(pair, 2)
        poll(2)

        @pl.when(pair < 2)
        def _():
            d_input(pair)

        poll(3)
        return carried

    for step in range(2):
        for piece in range(pieces):
            rings[2].gather_step(y_all, step, piece)
    lax.fori_loop(0, last, backward, 0)
    rings[3].scatter_step(part, held, 0)
    fetch(y_all, last)
    d_hidden(0, 2 * third)
    d_hidden(2 * third, whole)
    d_units(last, 0)
    rings[3].scatter_step(part, held, 1)
    d_units(last, 1)
    d_units(last, 2)
    rows_tile = stage.shape[1]
    tiles = 3 * whole // rows_tile
    upper_tiles = 2 * whole // rows_tile

    cut = units // 3

    def pieces_of(tile):
        for quarter in range(4):
            block = 4 * tile + quarter
            kind, slot, third = block // 12, (block // 3) % 4, block % 3
            source = stage.at[tile % 2, pl.ds(quarter * cut, cut)]
            rows = pl.ds(pl.multiple_of(kind * units + third * cut, cut), cut)
            sem = stage_sem.at[tile % 2, quarter]
            goal = terms_ref.at[slot, rows], other_ref.at[slot - 2, rows]
            there = functools.partial(
                remote, source, goal[1], sem, other_sem.at[tile, quarter], to_core
            )
            yield slot, functools.partial(pltpu.make_async_copy, source, goal[0], sem), there

    def keep(tile):
        for slot, here, there in pieces_of(tile):

            @pl.when(slot < 2)
            def _():
                here().start()

            @pl.when(slot >= 2)
            def _():
                there().start()

    def kept(tile):
        for slot, here, there in pieces_of(tile):

            @pl.when(slot < 2)
            def _():
                here().wait()

            @pl.when(slot >= 2)
            def _():
                there().wait_send()

    def grads(tile):
        @pl.when(tile >= 2)
        def _():
            kept(tile - 2)

        @pl.when(tile < upper_tiles)
        def _():
            columns = pl.ds(pl.multiple_of(tile * rows_tile, rows_tile), rows_tile)
            left = both[:, :, columns].reshape(chips * tok_rows, rows_tile)
            stage[tile % 2] = dot_tn(left, x_all[...].reshape(chips * tok_rows, width)).astype(bfloat)

        @pl.when(tile >= upper_tiles)
        def _():
            columns = pl.ds(
                pl.multiple_of((tile - upper_tiles) * rows_tile, rows_tile), rows_tile
            )
            left = hidden[:, :, columns].reshape(chips * tok_rows, rows_tile)
            stage[tile % 2] = dot_tn(left, y_all[...].reshape(chips * tok_rows, width)).astype(bfloat)

        keep(tile)

    d_input(2)

    def spread_back(step, carried):
        tile = 2 * (step - 3) + 2 * ((6 - step) // 4)
        rings[3].scatter_step(part, held, step, 0)

        @pl.when(step == 3)
        def _():
            d_input(3)

        @pl.when(step != 3)
        def _():
            grads(tile)

        rings[3].scatter_step(part, held, step, 1)

        @pl.when(step != 3)
        def _():
            grads(tile + 1)

        return carried

    lax.fori_loop(2, chips - 1, spread_back, 0)
    lax.fori_loop(8, tiles, lambda tile, carried: grads(tile) or carried, 0)
    rings[3].scatter_end(part, held, wide)
    d_norm, d_gain = norm_back(mid[...], scales_ref[2:3], wide[ours])
    d_gains_ref[2:3] = d_gain
    d_mid_ref[...] = dy_ref[...] + d_norm
    d_projected, d_gain = norm_back(projected_ref[...], scales_ref[1:2], d_mid_ref[...])
    d_gains_ref[1:2] = d_gain
    d_projected_ref[...] = d_projected.astype(bfloat)
    rings[2].finish(x_all.at[0, 0 : rings[0].size])
    rings[3].finish(x_all.at[0, 0 : rings[0].size])
    kept(tiles - 2)
    kept(tiles - 1)

    def gained(tile, carried):
        for slot, here, there in pieces_of(tile):

            @pl.when(slot >= 2)
            def _():
                there().wait_recv()

        return carried

    lax.fori_loop(0, tiles, gained, 0)


def feed_forward(resid_in, projected, grad_out, scales, shares, chips, ident):
    tok_rows, width = resid_in.shape
    units = shares[0].shape[0] // 3
    whole = 4 * units
    pieces = 2
    vmem = pl.BlockSpec(memory_space=pltpu.VMEM)
    anywhere = pl.BlockSpec(memory_space=pl.ANY)
    return pl.pallas_call(
        functools.partial(feed_kernel, chips, pieces),
        out_shape=(
            jax.ShapeDtypeStruct((tok_rows, width), single),
            jax.ShapeDtypeStruct((tok_rows, width), single),
            jax.ShapeDtypeStruct((tok_rows, width), bfloat),
            jax.ShapeDtypeStruct((4, width), single),
            jax.ShapeDtypeStruct((2, 3 * units, width), bfloat),
            jax.ShapeDtypeStruct((2, 3 * units, width), bfloat),
        ),
        in_specs=[vmem] * 4 + [anywhere] * 4,
        out_specs=(vmem, vmem, vmem, vmem, anywhere, anywhere),
        scratch_shapes=[
            pltpu.VMEM((3 * whole, width), bfloat),
            pltpu.VMEM((chips, tok_rows, width), bfloat),
            pltpu.VMEM((chips, tok_rows, width), bfloat),
            pltpu.VMEM((tok_rows, width), single),
            pltpu.VMEM((chips, tok_rows, 2 * whole), bfloat),
            pltpu.VMEM((chips, tok_rows, whole), bfloat),
            pltpu.VMEM((chips, tok_rows, width), bfloat),
            pltpu.VMEM((2, chips - 1, tok_rows // 2, width), bfloat),
            pltpu.VMEM((2 * tok_rows, width), bfloat),
            pltpu.VMEM((2 * tok_rows, width), single),
            pltpu.VMEM((2, whole // 3, width), bfloat),
            pltpu.SemaphoreType.DMA((4, 3)),
            pltpu.SemaphoreType.DMA((2,)),
            pltpu.SemaphoreType.DMA((2,)),
            pltpu.SemaphoreType.DMA((2, 4)),
            pltpu.SemaphoreType.DMA((9, 4)),
            pltpu.SemaphoreType.DMA((4, 2, pieces, chips - 1)),
            pltpu.SemaphoreType.DMA((4, 2, pieces, chips - 1)),
        ],
        compiler_params=pltpu.CompilerParams(
            collective_id=ident, has_side_effects=True, vmem_limit_bytes=63 * 2**20
        ),
        cost_estimate=cost(205),
    )(resid_in, projected, grad_out, scales, *shares)


def general_device(
    tokens,
    cotangent,
    gains,
    gains_first,
    gains_second,
    attn_weight,
    attn_first,
    attn_second,
    ffn_weight,
    ffn_first,
    ffn_second,
):
    devices = lax.axis_size("fsdp")
    chips = devices // 2
    side = lax.axis_index("head")
    place = lax.axis_index("fsdp")
    core, chip = place % 2, place // 2
    tok_rows = tokens.shape[1]
    super_rows = 4 * tok_rows
    seq_len = min(SEQ_LEN, super_rows * chips)
    share = attn_weight.shape[1]
    pairs = chips // 4
    width = tokens.shape[2]
    scale = 1.0 / math.sqrt(HD)

    def swap_core(value):
        return lax.ppermute(value, "fsdp", [(index, index ^ 1) for index in range(devices)])

    def swap_side(value):
        return lax.ppermute(value, "head", [(0, 1), (1, 0)])

    def in_order(own, other, index, axis):
        return jnp.where(
            index == 0, jnp.stack([own, other], axis), jnp.stack([other, own], axis)
        )

    def pick(value, index, axis=0):
        return lax.dynamic_index_in_dim(value, index, axis, keepdims=False)

    def quad_gather(value):
        value = in_order(value, swap_side(value), side, 0)
        value = in_order(value, swap_core(value), core, 0)
        return value.reshape((super_rows,) + value.shape[3:])

    def quad_scatter(partial):
        partial = partial.reshape(2, 2, tok_rows, width)
        mine = pick(partial, core) + swap_core(pick(partial, 1 - core).astype(bfloat)).astype(single)
        return pick(mine, side) + swap_side(pick(mine, 1 - side).astype(bfloat)).astype(single)

    scales = lax.all_gather(gains.astype(bfloat), ("head", "fsdp"), axis=1, tiled=True).astype(single)
    attn_low = attn_weight.astype(bfloat)
    ffn_low = ffn_weight.astype(bfloat).transpose(1, 0, 2)
    ffn_pair = jnp.concatenate([ffn_low, swap_side(ffn_low)], axis=1)

    ring_rows = ring_gather(attn_low.reshape(3 * share, width), chips, 0)
    ring_rows = ring_rows.reshape(2, 2, pairs, 3, share, width)

    def query_rows(slot):
        rows = ring_rows[:, :, :, slot]
        other = swap_core(pick(rows, 1 - core))
        return in_order(pick(rows, core), other, core, 2).reshape(2 * HD, width)

    def keyval_rows():
        rows = ring_rows[:, :, :, 1]
        other = swap_core(pick(rows, 1 - core, 1))
        return in_order(pick(rows, core, 1), other, core, 2).reshape(2 * HD, width)

    w_query, w_keyval, w_out = query_rows(0), keyval_rows(), query_rows(2)

    resid_in = tokens[0]
    grad_out = cotangent[0]
    normed_one = norm_scale(resid_in, scales[0]).astype(bfloat)
    normed_all = quad_gather(normed_one)
    positions = chip * super_rows + jnp.arange(super_rows, dtype=jnp.int32)
    angles = turn_angles(positions % seq_len, HD)
    query_raw = jnp.einsum("td,fd->tf", normed_all, w_query, preferred_element_type=single)
    keyval_raw = jnp.einsum("td,fd->tf", normed_all, w_keyval, preferred_element_type=single)
    query = rotate(query_raw.reshape(super_rows, 2, HD), angles, 1.0).astype(bfloat)
    key_angles = jnp.where(side == 0, angles, 0.0)
    keyval = rotate(keyval_raw.reshape(super_rows, 2, HD), key_angles, 1.0).astype(bfloat)
    keyval = in_order(pick(keyval, side, 1), swap_side(pick(keyval, 1 - side, 1)), side, 0)
    keyval_all = ring_gather(keyval.reshape(2 * super_rows, HD), chips, 1)
    keyval_all = keyval_all.reshape(chips, 2, super_rows, HD)
    key_all = keyval_all[:, 0].reshape(chips * super_rows, HD)
    value_all = keyval_all[:, 1].reshape(chips * super_rows, HD)

    key_pos = jnp.arange(chips * super_rows, dtype=jnp.int32)
    distance = positions[:, None] - key_pos[None, :]
    same_seq = (positions // seq_len)[:, None] == (key_pos // seq_len)[None, :]
    allowed = (distance >= 0) & (distance < WIN) & same_seq

    def score_block():
        raw = jnp.einsum("qgd,kd->gqk", query, key_all, preferred_element_type=single)
        bent = jnp.tanh(raw * (scale / softcap))
        return bent, jnp.where(allowed, jnp.exp(softcap * bent), 0.0)

    bent, powers = score_block()
    total = jnp.sum(powers, axis=-1, keepdims=True)
    attended = jnp.einsum(
        "gqk,kd->gqd", powers.astype(bfloat), value_all, preferred_element_type=single
    )
    attended = (attended / total).transpose(1, 0, 2).reshape(super_rows, 2 * HD).astype(bfloat)
    projected = quad_scatter(jnp.dot(attended, w_out, preferred_element_type=single))
    resid_mid = resid_in + norm_scale(projected, scales[1])
    normed_two = norm_scale(resid_mid, scales[2]).astype(bfloat)

    ffn_all = jnp.concatenate([ffn_pair, swap_core(ffn_pair)], axis=1)
    w_gate, w_up, w_down = ffn_all[0], ffn_all[1], ffn_all[2]
    ring_tokens = chips * tok_rows
    normed_ring = ring_gather(normed_two, chips, 2).reshape(ring_tokens, width)
    gate_part = jnp.einsum("td,rd->tr", normed_ring, w_gate, preferred_element_type=single)
    up_part = jnp.einsum("td,rd->tr", normed_ring, w_up, preferred_element_type=single)
    hidden = hidden_unit(gate_part, up_part).astype(bfloat)
    ffn_part = jnp.dot(hidden, w_down, preferred_element_type=single).astype(bfloat)
    ffn_acc = ring_scatter(ffn_part.reshape(chips, tok_rows, width), chips, 3)
    result = resid_mid + norm_scale(ffn_acc, scales[3])

    ignored, post_back = jax.vjp(norm_scale, ffn_acc, scales[3])
    d_ffn, d_gain3 = post_back(grad_out)
    d_ffn_ring = ring_gather(d_ffn.astype(bfloat), chips, 4).reshape(ring_tokens, width)
    d_hidden = jnp.einsum("td,rd->tr", d_ffn_ring, w_down, preferred_element_type=single)
    ignored, unit_back = jax.vjp(hidden_unit, gate_part, up_part)
    d_gate, d_up = unit_back(d_hidden)
    d_gate = d_gate.astype(bfloat)
    d_up = d_up.astype(bfloat)
    d_normed = jnp.dot(d_gate, w_gate, preferred_element_type=single)
    d_normed = (d_normed + jnp.dot(d_up, w_up, preferred_element_type=single)).astype(bfloat)
    d_normed_two = ring_scatter(d_normed.reshape(chips, tok_rows, width), chips, 5)

    def ffn_rows(left, right):
        return jnp.einsum("tr,td->rd", left, right, preferred_element_type=single)

    ffn_terms = jnp.stack(
        [ffn_rows(d_gate, normed_ring), ffn_rows(d_up, normed_ring), ffn_rows(hidden, d_ffn_ring)]
    )
    units = ffn_weight.shape[0]
    ffn_terms = ffn_terms.reshape(3, 2, 2, units, width)
    ffn_terms = ffn_terms[:, 0] + swap_core(ffn_terms[:, 1].astype(bfloat)).astype(single)
    grad_ffn = ffn_terms[:, 0] + swap_side(ffn_terms[:, 1].astype(bfloat)).astype(single)

    ignored, mid_back = jax.vjp(norm_scale, resid_mid, scales[2])
    d_mid_norm, d_gain2 = mid_back(d_normed_two)
    d_mid = grad_out + d_mid_norm
    ignored, proj_back = jax.vjp(norm_scale, projected, scales[1])
    d_projected, d_gain1 = proj_back(d_mid)
    d_proj_all = quad_gather(d_projected.astype(bfloat))
    d_attended = jnp.einsum("td,fd->tf", d_proj_all, w_out, preferred_element_type=single)
    d_attended = d_attended.astype(bfloat).reshape(super_rows, 2, HD)

    bent, powers = score_block()
    probs = powers / total
    d_probs = jnp.einsum("qgd,kd->gqk", d_attended, value_all, preferred_element_type=single)
    row_dot = jnp.sum(d_probs * probs, axis=-1, keepdims=True)
    d_raw = (probs * (d_probs - row_dot) * (1.0 - bent * bent)).astype(bfloat)
    d_query = jnp.einsum("gqk,kd->qgd", d_raw, key_all, preferred_element_type=single) * scale
    d_keys = jnp.einsum("gqk,qgd->kd", d_raw, query, preferred_element_type=single) * scale
    d_values = jnp.einsum(
        "gqk,qgd->kd", probs.astype(bfloat), d_attended, preferred_element_type=single
    )
    d_pieces = jnp.stack(
        [d_keys.reshape(chips, super_rows, HD), d_values.reshape(chips, super_rows, HD)], axis=1
    ).astype(bfloat)
    d_keyval = ring_scatter(d_pieces.reshape(chips, 2 * super_rows, HD), chips, 6)
    d_keyval = d_keyval.reshape(2, super_rows, HD).astype(bfloat)
    d_keyval = in_order(pick(d_keyval, side), swap_side(pick(d_keyval, 1 - side)), side, 1)
    d_query_raw = rotate(d_query, angles, -1.0).reshape(super_rows, 2 * HD).astype(bfloat)
    d_keyval_raw = rotate(d_keyval.astype(single), key_angles, -1.0)
    d_keyval_raw = d_keyval_raw.reshape(super_rows, 2 * HD).astype(bfloat)
    d_normed_one = jnp.dot(d_query_raw, w_query, preferred_element_type=single)
    d_normed_one = d_normed_one + jnp.dot(d_keyval_raw, w_keyval, preferred_element_type=single)
    d_normed_one = quad_scatter(d_normed_one)
    ignored, first_back = jax.vjp(norm_scale, resid_in, scales[0])
    d_in_norm, d_gain0 = first_back(d_normed_one)
    tokens_grad = d_mid + d_in_norm

    def attn_rows(left, right):
        rows = jnp.einsum("tf,td->fd", left, right, preferred_element_type=single).astype(bfloat)
        return rows.reshape(2, pairs, 2, share, width)

    term_query = attn_rows(d_query_raw, normed_all)
    term_keyval = attn_rows(d_keyval_raw, normed_all)
    term_out = attn_rows(attended, d_proj_all)

    def to_core(term, axis):
        return in_order(pick(term, core, 2), swap_core(pick(term, 1 - core, 2)), core, axis)

    terms = jnp.stack([to_core(term_query, 0), to_core(term_keyval, 1), to_core(term_out, 0)], axis=3)
    grad_attn = ring_scatter(terms.reshape(chips, 3 * share, width), chips, 7)
    grad_attn = grad_attn.reshape(3, share, width)
    term_gain = jnp.stack([d_gain0, d_gain1, d_gain2, d_gain3])
    grad_gain = lax.psum_scatter(term_gain, ("head", "fsdp"), scatter_dimension=1, tiled=True)

    gains_first_new, gains_second_new, gains_new = adamw(
        gains, gains_first, gains_second, grad_gain, rate_gain, 0.0
    )
    attn_first_new, attn_second_new, attn_weight_new = adamw(
        attn_weight, attn_first, attn_second, grad_attn, rate_matrix, decay_matrix
    )
    ffn_first_new, ffn_second_new, ffn_weight_new = adamw(
        ffn_weight, ffn_first, ffn_second, grad_ffn.transpose(1, 0, 2), rate_matrix, decay_matrix
    )
    return (
        result[None],
        tokens_grad[None],
        gains_first_new,
        gains_second_new,
        gains_new,
        attn_first_new,
        attn_second_new,
        attn_weight_new,
        ffn_first_new,
        ffn_second_new,
        ffn_weight_new,
    )


def step_kernel(
    tiles,
    weight_ref,
    first_ref,
    second_ref,
    own_ref,
    side_ref,
    weight_two_ref,
    first_two_ref,
    second_two_ref,
    grad_two_ref,
    first_out,
    second_out,
    weight_out,
    first_two_out,
    second_two_out,
    weight_two_out,
):
    index = pl.program_id(0)

    @pl.when(index < tiles)
    def _():
        grad = own_ref[...].astype(single) + side_ref[...].astype(single)
        first_out[...], second_out[...], weight_out[...] = adamw(
            weight_ref[...], first_ref[...], second_ref[...], grad, rate_matrix, decay_matrix
        )

    @pl.when(index >= tiles)
    def _():
        first_two_out[...], second_two_out[...], weight_two_out[...] = adamw(
            weight_two_ref[...],
            first_two_ref[...],
            second_two_ref[...],
            grad_two_ref[...],
            rate_matrix,
            decay_matrix,
        )


def step_weights(state, own, side, state_two, grad_two):
    rows, width = state[0].shape
    rows_two = grad_two.shape[0]
    size = 96
    tiles, tiles_two = rows // size, rows_two // size
    block = pl.BlockSpec((size, width), lambda index: (jnp.minimum(index, tiles - 1), 0))
    block_two = pl.BlockSpec((size, width), lambda index: (jnp.maximum(index - tiles, 0), 0))
    return pl.pallas_call(
        functools.partial(step_kernel, tiles),
        grid=(tiles + tiles_two,),
        out_shape=(jax.ShapeDtypeStruct((rows, width), single),) * 3
        + (jax.ShapeDtypeStruct((rows_two, width), single),) * 3,
        in_specs=[block] * 5 + [block_two] * 4,
        out_specs=(block,) * 3 + (block_two,) * 3,
        compiler_params=pltpu.CompilerParams(vmem_limit_bytes=62 * 2**20),
        cost_estimate=cost(20),
    )(*state, own, side, *state_two, grad_two)


def per_device(
    tokens,
    cotangent,
    gains,
    gains_first,
    gains_second,
    attn_weight,
    attn_first,
    attn_second,
    ffn_weight,
    ffn_first,
    ffn_second,
):
    devices = lax.axis_size("fsdp")
    chips = devices // 2
    side = lax.axis_index("head")
    place = lax.axis_index("fsdp")
    tok_rows = tokens.shape[1]
    share = attn_weight.shape[1]
    width = tokens.shape[2]
    gain_columns = gains.shape[1]
    gain_start = (side * devices + place) * gain_columns

    units = ffn_weight.shape[0]

    def flat(value):
        return value.transpose(1, 0, 2).reshape(3 * units, width)

    ffn_wide = flat(ffn_weight)
    resid_in = tokens[0]
    grad_out = cotangent[0]
    gains_placed = lax.dynamic_update_slice(
        jnp.zeros((4, width), single), gains, (0, gain_start)
    )
    halfway = HD // 2
    pace = jnp.asarray(
        10000.0 ** (-2.0 * np.arange(halfway, dtype=np.float64) / HD)[None, :], dtype=single
    )
    made = front(attn_weight, gains_placed, resid_in, pace, ffn_wide, chips, 0)
    attn_rows, scales, normed_all, query, keyval, attended, inverse, projected = made[:8]
    turns = made[8:12]
    own_units, core_units, side_units, diag_units = made[12:]
    result, d_mid, d_proj_low, gain_rows, terms_own, terms_other = feed_forward(
        resid_in,
        projected,
        grad_out,
        scales,
        (own_units, side_units, core_units, diag_units),
        chips,
        1,
    )
    grad_attn, tokens_grad, gain_total, terms_sent, terms_side, terms_mine = tail(
        d_proj_low,
        query,
        keyval,
        attended,
        inverse,
        attn_rows,
        normed_all,
        turns,
        (resid_in, d_mid, scales, gain_rows),
        terms_own,
        terms_other,
        chips,
        2,
    )
    grad_gain = lax.dynamic_slice(gain_total, (0, gain_start), gains.shape)

    gains_first_new, gains_second_new, gains_new = adamw(
        gains, gains_first, gains_second, grad_gain, rate_gain, 0.0
    )
    def rows_of(value):
        return value.reshape(3 * share, width)

    stepped = step_weights(
        (ffn_wide, flat(ffn_first), flat(ffn_second)),
        terms_mine,
        terms_side,
        (rows_of(attn_weight), rows_of(attn_first), rows_of(attn_second)),
        grad_attn,
    )
    ffn_first_new, ffn_second_new, ffn_weight_new = (
        value.reshape(3, units, width).transpose(1, 0, 2) for value in stepped[:3]
    )
    attn_first_new, attn_second_new, attn_weight_new = (
        value.reshape(3, share, width) for value in stepped[3:]
    )
    return (
        result[None],
        tokens_grad[None],
        gains_first_new,
        gains_second_new,
        gains_new,
        attn_first_new,
        attn_second_new,
        attn_weight_new,
        ffn_first_new,
        ffn_second_new,
        ffn_weight_new,
    )


def solution(mesh):
    by_token = P("fsdp", "head", None)
    by_column = P(None, ("head", "fsdp"))
    by_row = P(None, ("head", "fsdp"), None)
    by_unit = P(("head", "fsdp"), None, None)
    placed = (by_token,) * 2 + (by_column,) * 3 + (by_row,) * 3 + (by_unit,) * 3
    body = per_device if mesh.shape["fsdp"] == 16 else general_device
    return jax.shard_map(
        body, mesh=mesh, in_specs=placed, out_specs=placed, check_vma=False
    )
```

profile of v0, /device:TPU:0, one launch (start us, length us, event | category | flops | bytes accessed | tf_op | source)
XLA Modules:
  0.0 533.8 jit_solution(1868745127056049827)
XLA Ops:
  0.7 0.8 dynamic_update_slice.3.gains_ref
  1.5 0.0 copy-start.2
  1.5 0.6 copy-done.2
  2.1 149.1 %shard_map.203 = (bf16[3,512,2304]{2,1,0:T(8,128)(2,1)}, f32[4,2304]{1,0:T(4,128)}, bf16[2,2,128,2304]{3,2,1,0:T(8,128)(2,1)}, bf16[2,512,256]{2,1,0:T(8,128)(2,...) custom-call(f32[3,64,2304]{2,1,0:T(8,128)} %own_ref.1, ...), custom_call_target="tpu_custom_call" | custom-call | flops 140000002048 | tf_op jit(solution)/shard_map/pallas_call | solution.py:869
  151.2 198.7 %shard_map.204 = (f32[128,2304]{1,0:T(8,128)}, f32[128,2304]{1,0:T(8,128)}, bf16[128,2304]{1,0:T(8,128)(2,1)}, f32[4,2304]{1,0:T(4,128)}, bf16[2,864,2304]{2,1,0:T(8,128)(2,1)}, /*index=5*/bf16[2,864,2304]{2,1,0:T(8,128)(2,1)}) custom-call(f32[128,2304]{1,0:T(8,128)} %bitcast.39, f32[128,2304]{1,0:T(8,128)} %get-tuple-element.44.projected_ref, ...), custom_call_target="tpu_custom_call" | custom-call | flops 204999999488 | tf_op jit(solution)/shard_map/pallas_call | solution.py:1744
  349.9 0.0 copy-start.3
  349.9 0.0 copy-start.4
  349.9 0.0 copy-start.5
  349.9 150.5 %shard_map.205 = (f32[192,2304]{1,0:T(8,128)}, f32[128,2304]{1,0:T(8,128)}, f32[4,2304]{1,0:T(4,128)}, bf16[864,2304]{1,0:T(8,128)(2,1)}, bf16[864,2304]{1,0:T(8,128)(2,1)}, /*index=5*/bf16[864,2304]{1,0:T(8,128)(2,1)}) custom-call(bf16[128,2304]{1,0:T(8,128)(2,1)} %get-tuple-element.51.d_proj_ref, bf16[2,512,256]{2,1,0:T(8,128)(2,1)} %get-tuple-element.52.query_ref, ...), custom_call_target="tpu_custom_call" | custom-call | flops 160000000000 | tf_op jit(solution)/shard_map/pallas_call | solution.py:1325
  500.4 0.0 copy-done.3
  500.4 0.0 copy-done.4
  500.4 0.0 copy-done.5
  500.4 1.4 multiply_subtract_fusion
  501.8 0.0 copy-start
  501.8 28.9 %shard_map.206 = (f32[864,2304]{1,0:T(8,128)}, f32[864,2304]{1,0:T(8,128)}, f32[864,2304]{1,0:T(8,128)}, f32[192,2304]{1,0:T(8,128)}, f32[192,2304]{1,0:T(8,128)}, /*index=5*/f32[192,2304]{1,0:T(8,128)}) custom-call(f32[864,2304]{1,0:T(8,128)} %bitcast.31, f32[864,2304]{1,0:T(8,128)} %bitcast.32, f32[864,2304]{1,0:T(8,128)} %bitcast.33, ...), custom_call_target="tpu_custom_call" | custom-call | flops 20000000000 | tf_op jit(solution)/shard_map/pallas_call | solution.py:2046
  530.6 0.0 copy-start.1
  530.6 0.0 copy-done
  530.7 1.0 copy.26
  531.7 0.7 copy-done.1
  532.3 1.0 copy.27
  (1 shorter events, 0.0 us)
Async XLA Ops:
  1.5 0.6 copy-start.2
  349.9 150.5 %copy-start.3 = (f32[4,72]{1,0:T(4,128)S(1)}, f32[4,72]{1,0:T(4,128)}, u32[]{:S(2)}) copy-start(f32[4,72]{1,0:T(4,128)} %param.14) | copy-start | bytes 3460
  349.9 150.5 %copy-start.4 = (f32[4,72]{1,0:T(4,128)S(1)}, f32[4,72]{1,0:T(4,128)}, u32[]{:S(2)}) copy-start(f32[4,72]{1,0:T(4,128)} %param.16) | copy-start | bytes 3460
  349.9 150.5 %copy-start.5 = (f32[4,72]{1,0:T(4,128)S(1)}, f32[4,72]{1,0:T(4,128)}, u32[]{:S(2)}) copy-start(f32[4,72]{1,0:T(4,128)} %param.15) | copy-start | bytes 3460
  501.8 28.9 %copy-start = (f32[128,2304]{1,0:T(8,128)S(1)}, f32[128,2304]{1,0:T(8,128)}, u32[]{:S(2)}) copy-start(f32[128,2304]{1,0:T(8,128)} %get-tuple-element.50) | copy-start | bytes 3538948
  530.6 1.7 copy-start.1
where the time goes:
time: 539 us; the launch traced here: 534 us
  Pallas kernels  527 us (98%)
    pallas_call x1, Pallas kernels, feed_forward(): pl.pallas_call(functools.partial(feed_kernel, chips, pieces), out_shape=(...  199 us
    pallas_call x1, Pallas kernels, tail(): pl.pallas_call(functools.partial(tail_kernel, chips), out_shape=(jax.Shap...  150 us
    pallas_call x1, Pallas kernels, front(): pl.pallas_call(functools.partial(front_kernel, chips, cuts), out_shape=(j...  149 us
    pallas_call x1, Pallas kernels, step_weights(): pl.pallas_call(functools.partial(step_kernel, tiles), grid=(tiles + tiles...  28.9 us

commit v1 on v0

--- a/solution.py
+++ b/solution.py
@@ -717,7 +717,6 @@
     cast(6, casts)
     cast_store(casts - 2).wait()
     cast_store(casts - 1).wait()
-    bulk_core.start()
     along.wait()
     across.start()
     bulk_side(1).start()
@@ -743,6 +742,7 @@
     swap = quad_copy(both.at[1 - side], keyval_ref.at[chip, side], 2, to_side)
     swap.start()
     bulk_side(2).start()
+    bulk_core.start()
     for part in range(2):
         bulk_side(part).wait_recv()
         bulk_diag(part).start()
@@ -1012,12 +1012,15 @@
     def quad_copy(source, target, index, device):
         return remote(source, target, quad_send.at[index], quad_recv.at[index], device)
 
-    def bulk(kind):
+    cuts = (0, 320, 640, units_ref.shape[0])
+
+    def bulk(part):
+        rows = pl.ds(cuts[part], cuts[part + 1] - cuts[part])
         return remote(
-            units_ref.at[pl.ds(kind * (units_ref.shape[0] // 3), units_ref.shape[0] // 3)],
-            units_got_ref.at[pl.ds(kind * (units_ref.shape[0] // 3), units_ref.shape[0] // 3)],
-            bulk_send.at[kind],
-            bulk_recv.at[kind],
+            units_ref.at[rows],
+            units_got_ref.at[rows],
+            bulk_send.at[part],
+            bulk_recv.at[part],
             to_side,
         )
 
@@ -1229,7 +1232,6 @@
         place(0, head, False)
     rings[0].scatter_step(parts.at[0], held.at[0], 0)
     swap.wait()
-    bulk(2).start()
     swapped[side] = swapped[2 + side]
     for head in range(2):
         turned = turn(swapped[head].astype(single), key_cosine_ref[...], -key_sine_ref[...])
@@ -1271,6 +1273,7 @@
             given = out_rows[0, core, other].astype(single) + across_got[other].astype(single)
             along_put[...] = given.astype(bfloat)
             along.start()
+            bulk(2).start()
             tokens_ref[...] = out_rows[0, core, mine].astype(single) + across_got[mine].astype(single)
 
         @pl.when(step == 4)

time: 539 us -> 540 us (level)
  no operation moved by 1% of the time
where the time goes in v1:
time: 540 us; the launch traced here: 535 us
  Pallas kernels  528 us (98%)
    pallas_call x1, Pallas kernels, feed_forward(): pl.pallas_call(functools.partial(feed_kernel, chips, pieces), out_shape=(...  199 us
    pallas_call x1, Pallas kernels, tail(): pl.pallas_call(functools.partial(tail_kernel, chips), out_shape=(jax.Shap...  152 us
    pallas_call x1, Pallas kernels, front(): pl.pallas_call(functools.partial(front_kernel, chips, cuts), out_shape=(j...  149 us
    pallas_call x1, Pallas kernels, step_weights(): pl.pallas_call(functools.partial(step_kernel, tiles), grid=(tiles + tiles...  28.9 us

profile of v1, /device:TPU:0, one launch (start us, length us, event | category | flops | bytes accessed | tf_op | source)
XLA Modules:
  0.0 535.1 jit_solution(11277148794750882180)
XLA Ops:
  0.7 0.8 dynamic_update_slice.3.gains_ref
  1.5 0.0 copy-start.2
  1.5 0.6 copy-done.2
  2.1 149.0 %shard_map.203 = (bf16[3,512,2304]{2,1,0:T(8,128)(2,1)}, f32[4,2304]{1,0:T(4,128)}, bf16[2,2,128,2304]{3,2,1,0:T(8,128)(2,1)}, bf16[2,512,256]{2,1,0:T(8,128)(2,...) custom-call(f32[3,64,2304]{2,1,0:T(8,128)} %own_ref.1, ...), custom_call_target="tpu_custom_call" | custom-call | flops 140000002048 | tf_op jit(solution)/shard_map/pallas_call | solution.py:869
  151.1 198.8 %shard_map.204 = (f32[128,2304]{1,0:T(8,128)}, f32[128,2304]{1,0:T(8,128)}, bf16[128,2304]{1,0:T(8,128)(2,1)}, f32[4,2304]{1,0:T(4,128)}, bf16[2,864,2304]{2,1,0:T(8,128)(2,1)}, /*index=5*/bf16[2,864,2304]{2,1,0:T(8,128)(2,1)}) custom-call(f32[128,2304]{1,0:T(8,128)} %bitcast.39, f32[128,2304]{1,0:T(8,128)} %get-tuple-element.44.projected_ref, ...), custom_call_target="tpu_custom_call" | custom-call | flops 204999999488 | tf_op jit(solution)/shard_map/pallas_call | solution.py:1747
  349.9 0.0 copy-start.3
  349.9 0.0 copy-start.4
  349.9 0.0 copy-start.5
  349.9 151.8 %shard_map.205 = (f32[192,2304]{1,0:T(8,128)}, f32[128,2304]{1,0:T(8,128)}, f32[4,2304]{1,0:T(4,128)}, bf16[864,2304]{1,0:T(8,128)(2,1)}, bf16[864,2304]{1,0:T(8,128)(2,1)}, /*index=5*/bf16[864,2304]{1,0:T(8,128)(2,1)}) custom-call(bf16[128,2304]{1,0:T(8,128)(2,1)} %get-tuple-element.51.d_proj_ref, bf16[2,512,256]{2,1,0:T(8,128)(2,1)} %get-tuple-element.52.query_ref, ...), custom_call_target="tpu_custom_call" | custom-call | flops 160000000000 | tf_op jit(solution)/shard_map/pallas_call | solution.py:1328
  501.7 0.0 copy-done.3
  501.7 0.0 copy-done.4
  501.7 0.0 copy-done.5
  501.7 1.4 multiply_subtract_fusion
  503.1 0.0 copy-start
  503.1 28.9 %shard_map.206 = (f32[864,2304]{1,0:T(8,128)}, f32[864,2304]{1,0:T(8,128)}, f32[864,2304]{1,0:T(8,128)}, f32[192,2304]{1,0:T(8,128)}, f32[192,2304]{1,0:T(8,128)}, /*index=5*/f32[192,2304]{1,0:T(8,128)}) custom-call(f32[864,2304]{1,0:T(8,128)} %bitcast.31, f32[864,2304]{1,0:T(8,128)} %bitcast.32, f32[864,2304]{1,0:T(8,128)} %bitcast.33, ...), custom_call_target="tpu_custom_call" | custom-call | flops 20000000000 | tf_op jit(solution)/shard_map/pallas_call | solution.py:2049
  531.9 0.0 copy-start.1
  532.0 0.0 copy-done
  532.0 1.0 copy.26
  533.0 0.7 copy-done.1
  533.6 1.0 copy.27
  (1 shorter events, 0.0 us)
Async XLA Ops:
  1.5 0.6 copy-start.2
  349.9 151.8 %copy-start.3 = (f32[4,72]{1,0:T(4,128)S(1)}, f32[4,72]{1,0:T(4,128)}, u32[]{:S(2)}) copy-start(f32[4,72]{1,0:T(4,128)} %param.14) | copy-start | bytes 3460
  349.9 151.8 %copy-start.4 = (f32[4,72]{1,0:T(4,128)S(1)}, f32[4,72]{1,0:T(4,128)}, u32[]{:S(2)}) copy-start(f32[4,72]{1,0:T(4,128)} %param.16) | copy-start | bytes 3460
  349.9 151.8 %copy-start.5 = (f32[4,72]{1,0:T(4,128)S(1)}, f32[4,72]{1,0:T(4,128)}, u32[]{:S(2)}) copy-start(f32[4,72]{1,0:T(4,128)} %param.15) | copy-start | bytes 3460
  503.1 28.9 %copy-start = (f32[128,2304]{1,0:T(8,128)S(1)}, f32[128,2304]{1,0:T(8,128)}, u32[]{:S(2)}) copy-start(f32[128,2304]{1,0:T(8,128)} %get-tuple-element.50) | copy-start | bytes 3538948
  531.9 1.7 copy-start.1

commit v2 on v0

--- a/solution.py
+++ b/solution.py
@@ -756,7 +756,7 @@
     sums[...] = jnp.zeros_like(sums)
     swap.wait()
 
-    def block(way, owner):
+    def block(way, owner, own):
         part = tokens // 2
         key = keyval_ref[owner, 0, way * part : way * part + part]
         val = keyval_ref[owner, 1, way * part : way * part + part]
@@ -766,7 +766,9 @@
 
         def one_head(head, carried):
             bent = jnp.tanh(dot_nt(query_ref[head], key) * (scale / softcap))
-            powers = jnp.where(allowed, jnp.exp(softcap * bent), 0.0)
+            powers = jnp.exp2((softcap / math.log(2.0)) * bent)
+            if own:
+                powers = jnp.where(allowed, powers, 0.0)
             sums[head] += powers[:, : part // 2] + powers[:, part // 2 :]
             total[head] += dot_nn(powers.astype(bfloat), val)
             return carried
@@ -788,9 +790,13 @@
         for way in range(2):
             owner = owner_of(way, step)
 
-            @pl.when(owner <= chip)
+            @pl.when(owner < chip)
             def _():
-                block(way, owner)
+                block(way, owner, False)
+
+            @pl.when(step == 0)
+            def _():
+                block(way, chip, True)
 
             if way == 0:
 
@@ -1123,7 +1129,7 @@
         out_rows[slot, head] = dot_tn(left, right).astype(bfloat)
         place(slot, head, True)
 
-    def block(way, owner):
+    def block(way, owner, own):
         key = keyval_ref[owner, 0, way * half : way * half + half]
         val = keyval_ref[owner, 1, way * half : way * half + half]
         row = lax.broadcasted_iota(jnp.int32, (tokens, half), 0)
@@ -1134,7 +1140,9 @@
             bent = jnp.tanh(dot_nt(query_ref[head], key) * (scale / softcap))
             inverse = jnp.concatenate([inverse_ref[head]] * (half // 128), axis=1)
             row_dot = jnp.concatenate([delta[head]] * (half // 128), axis=1)
-            probs = jnp.where(allowed, jnp.exp(softcap * bent), 0.0) * inverse
+            probs = jnp.exp2((softcap / math.log(2.0)) * bent) * inverse
+            if own:
+                probs = jnp.where(allowed, probs, 0.0)
             d_probs = dot_nt(d_out[head], val)
             d_scores = (probs * (d_probs - row_dot) * (1.0 - bent * bent)).astype(bfloat)
             d_block[way, 0] += dot_tn(d_scores, query_ref[head]) * scale
@@ -1158,7 +1166,7 @@
 
     early = 3
 
-    def key_blocks(step):
+    def key_blocks(step, own=False):
         for way in range(2):
             owner = ring.owner(way, step + 1)
             d_block[way] = jnp.zeros(d_block.shape[1:], single)
@@ -1168,9 +1176,13 @@
                 def _():
                     out_ring.scatter_step(out_parts, out_held, step - early)
 
-            @pl.when(owner <= chip)
-            def _():
-                block(way, owner)
+            if own:
+                block(way, chip, True)
+            else:
+
+                @pl.when(owner < chip)
+                def _():
+                    block(way, owner, False)
 
     def key_body(step, carried):
         key_blocks(step)
@@ -1196,7 +1208,7 @@
 
         @pl.when(step == early - 1)
         def _():
-            key_blocks(chips - 1)
+            key_blocks(chips - 1, True)
             for way in range(2):
                 for kind in range(2):
                     rows = slice(way * half, way * half + half)

time: 539 us -> 538 us (level)
  no operation moved by 1% of the time
where the time goes in v2:
time: 538 us; the launch traced here: 533 us
  Pallas kernels  526 us (98%)
    pallas_call x1, Pallas kernels, feed_forward(): pl.pallas_call(functools.partial(feed_kernel, chips, pieces), out_shape=(...  199 us
    pallas_call x1, Pallas kernels, tail(): pl.pallas_call(functools.partial(tail_kernel, chips), out_shape=(jax.Shap...  150 us
    pallas_call x1, Pallas kernels, front(): pl.pallas_call(functools.partial(front_kernel, chips, cuts), out_shape=(j...  149 us
    pallas_call x1, Pallas kernels, step_weights(): pl.pallas_call(functools.partial(step_kernel, tiles), grid=(tiles + tiles...  28.9 us

profile of v2, /device:TPU:0, one launch (start us, length us, event | category | flops | bytes accessed | tf_op | source)
XLA Modules:
  0.0 532.9 jit_solution(6241646187297314168)
XLA Ops:
  0.7 0.8 dynamic_update_slice.3.gains_ref
  1.5 0.0 copy-start.2
  1.5 0.6 copy-done.2
  2.1 149.0 %shard_map.203 = (bf16[3,512,2304]{2,1,0:T(8,128)(2,1)}, f32[4,2304]{1,0:T(4,128)}, bf16[2,2,128,2304]{3,2,1,0:T(8,128)(2,1)}, bf16[2,512,256]{2,1,0:T(8,128)(2,...) custom-call(f32[3,64,2304]{2,1,0:T(8,128)} %own_ref.1, ...), custom_call_target="tpu_custom_call" | custom-call | flops 140000002048 | tf_op jit(solution)/shard_map/pallas_call | solution.py:875
  151.1 198.9 %shard_map.204 = (f32[128,2304]{1,0:T(8,128)}, f32[128,2304]{1,0:T(8,128)}, bf16[128,2304]{1,0:T(8,128)(2,1)}, f32[4,2304]{1,0:T(4,128)}, bf16[2,864,2304]{2,1,0:T(8,128)(2,1)}, /*index=5*/bf16[2,864,2304]{2,1,0:T(8,128)(2,1)}) custom-call(f32[128,2304]{1,0:T(8,128)} %bitcast.39, f32[128,2304]{1,0:T(8,128)} %get-tuple-element.44.projected_ref, ...), custom_call_target="tpu_custom_call" | custom-call | flops 204999999488 | tf_op jit(solution)/shard_map/pallas_call | solution.py:1756
  350.1 0.0 copy-start.3
  350.1 0.0 copy-start.4
  350.1 0.0 copy-start.5
  350.1 149.7 %shard_map.205 = (f32[192,2304]{1,0:T(8,128)}, f32[128,2304]{1,0:T(8,128)}, f32[4,2304]{1,0:T(4,128)}, bf16[864,2304]{1,0:T(8,128)(2,1)}, bf16[864,2304]{1,0:T(8,128)(2,1)}, /*index=5*/bf16[864,2304]{1,0:T(8,128)(2,1)}) custom-call(bf16[128,2304]{1,0:T(8,128)(2,1)} %get-tuple-element.51.d_proj_ref, bf16[2,512,256]{2,1,0:T(8,128)(2,1)} %get-tuple-element.52.query_ref, ...), custom_call_target="tpu_custom_call" | custom-call | flops 160000000000 | tf_op jit(solution)/shard_map/pallas_call | solution.py:1337
  499.8 0.0 copy-done.3
  499.8 0.0 copy-done.4
  499.8 0.0 copy-done.5
  499.8 1.4 multiply_subtract_fusion
  501.2 0.0 copy-start
  501.2 28.9 %shard_map.206 = (f32[864,2304]{1,0:T(8,128)}, f32[864,2304]{1,0:T(8,128)}, f32[864,2304]{1,0:T(8,128)}, f32[192,2304]{1,0:T(8,128)}, f32[192,2304]{1,0:T(8,128)}, /*index=5*/f32[192,2304]{1,0:T(8,128)}) custom-call(f32[864,2304]{1,0:T(8,128)} %bitcast.31, f32[864,2304]{1,0:T(8,128)} %bitcast.32, f32[864,2304]{1,0:T(8,128)} %bitcast.33, ...), custom_call_target="tpu_custom_call" | custom-call | flops 20000000000 | tf_op jit(solution)/shard_map/pallas_call | solution.py:2058
  530.0 0.0 copy-start.1
  530.0 0.0 copy-done
  530.0 1.0 copy.26
  531.1 0.7 copy-done.1
  531.7 1.0 copy.27
  (1 shorter events, 0.0 us)
Async XLA Ops:
  1.5 0.6 copy-start.2
  350.1 149.7 %copy-start.3 = (f32[4,72]{1,0:T(4,128)S(1)}, f32[4,72]{1,0:T(4,128)}, u32[]{:S(2)}) copy-start(f32[4,72]{1,0:T(4,128)} %param.14) | copy-start | bytes 3460
  350.1 149.7 %copy-start.4 = (f32[4,72]{1,0:T(4,128)S(1)}, f32[4,72]{1,0:T(4,128)}, u32[]{:S(2)}) copy-start(f32[4,72]{1,0:T(4,128)} %param.16) | copy-start | bytes 3460
  350.1 149.7 %copy-start.5 = (f32[4,72]{1,0:T(4,128)S(1)}, f32[4,72]{1,0:T(4,128)}, u32[]{:S(2)}) copy-start(f32[4,72]{1,0:T(4,128)} %param.15) | copy-start | bytes 3460
  501.2 28.9 %copy-start = (f32[128,2304]{1,0:T(8,128)S(1)}, f32[128,2304]{1,0:T(8,128)}, u32[]{:S(2)}) copy-start(f32[128,2304]{1,0:T(8,128)} %get-tuple-element.50) | copy-start | bytes 3538948
  530.0 1.7 copy-start.1
